TPU v7x, 256 devices: a whole 4x4x8 slice. The times are simulated.
256 devices in a mesh: row: 8 (over y_lo, x), col: 32 (over z, y_hi, core).
Axes of the slice: x: 4, y: 4 (y_hi: 2, y_lo: 2; y = y_hi * 2 + y_lo), z: 8, core: 2. Of those that a mesh axis runs over, the one named last changes fastest.
Arguments:
- left_features: bfloat16 [32, 2048, 320], P('row', 'col'), may hold values from -6 to 6
- right_features: bfloat16 [32, 2048, 320], P('row', 'col'), may hold values from -6 to 6
- conv_weight: bfloat16 [3, 3, 3, 40, 32], replicated, may hold values from -0.1875 to 0.1875
- cotangent: bfloat16 [24, 32, 2048, 32], P(None, 'row', 'col'), may hold values from -6 to 6
Outputs:
- cost_output: bfloat16 [24, 32, 2048, 32], P(None, 'row', 'col')
- weight_grad: float32 [3, 3, 3, 40, 32], replicated
- left_grad: bfloat16 [32, 2048, 320], P('row', 'col')
- right_grad: bfloat16 [32, 2048, 320], P('row', 'col')
All inputs are finite; a program needn't handle non-finite values.
Results may differ from a plain program's by a relative error of at most 0.0049.
Values may be sent and summed in bfloat16 or wider, within the bound.
A program may use at most 128 MiB of HBM per device.

v0:
```python
import math

import jax
import jax.numpy as jnp
from jax import lax
from jax.sharding import PartitionSpec as P

DISP = 24
STEP = 4


DIMS = ("NDHWC", "DHWIO", "NDHWC")
KERNEL_DIMS = ("CDHWN", "IDHWO", "NDHWC")


def shifted_2(block, axis, distance):
    devices = range(lax.axis_size(axis))
    route = [(i - distance, i) for i in devices if i - distance in devices]
    return lax.ppermute(block, axis, route)


def with_halo(cells, sides, width):
    for axis, dim in sides:
        count = lax.axis_size(axis)
        ends = count - 1
        head = lax.slice_in_dim(cells, 0, width, axis=dim)
        tail = lax.slice_in_dim(cells, cells.shape[dim] - width, cells.shape[dim], axis=dim)
        cells = jnp.concatenate(
            [
                lax.ppermute(tail, axis, [(i, (i + 1) % count) for i in range(ends)]),
                cells,
                lax.ppermute(head, axis, [((i + 1) % count, i) for i in range(ends)]),
            ],
            axis=dim,
        )
    return cells


def conv_valid(padded_input, kernel):
    return lax.conv_general_dilated(
        padded_input[None],
        kernel,
        (1, 1, 1),
        ((1, 1), (0, 0), (0, 0)),
        dimension_numbers=DIMS,
        preferred_element_type=jnp.float32,
    )[0]


def on_device(left_features, right_features, conv_weight, cotangent):
    tile_rows, tile_cols, channels = left_features.shape
    groups = conv_weight.shape[3]
    group_size = channels // groups
    reach_cols = STEP * (DISP - 1)
    hop_count = -(-reach_cols // tile_cols)
    band_base = hop_count * tile_cols
    band_width = band_base + tile_cols
    pieces = [right_features]
    carried = right_features
    for hop_index in range(hop_count):
        carried = shifted_2(carried, "col", 1)
        pieces.insert(0, carried)
    right_band = jnp.concatenate(pieces, axis=1)
    group_table = (
        jnp.arange(channels)[:, None] // group_size == jnp.arange(groups)[None, :]
    ).astype(jnp.float32)
    left_float = left_features.astype(jnp.float32)
    planes = []
    for disp_index in range(DISP):
        band_start = band_base - STEP * disp_index
        shifted = right_band[:, band_start : band_start + tile_cols].astype(jnp.float32)
        planes.append(
            jnp.einsum(
                "hwc,cg->hwg", left_float * shifted, group_table, precision=lax.Precision.HIGHEST
            )
        )
    volume = (jnp.stack(planes) / group_size).astype(jnp.bfloat16)
    padded_volume = with_halo(volume, (("row", 1), ("col", 2)), 1)
    output = conv_valid(padded_volume, conv_weight).astype(jnp.bfloat16)
    padded_cotangent = with_halo(cotangent, (("row", 1), ("col", 2)), 1)
    flipped = jnp.transpose(conv_weight[::-1, ::-1, ::-1], (0, 1, 2, 4, 3))
    grad_volume = conv_valid(padded_cotangent, flipped).astype(jnp.bfloat16)
    full_pad = jnp.pad(padded_volume, ((1, 1), (0, 0), (0, 0), (0, 0)))
    kernel_raw = lax.conv_general_dilated(
        full_pad[None],
        cotangent[None],
        (1, 1, 1),
        ((0, 0), (0, 0), (0, 0)),
        dimension_numbers=KERNEL_DIMS,
        preferred_element_type=jnp.float32,
    )
    local_grad = jnp.transpose(kernel_raw, (1, 2, 3, 0, 4))
    total_cells = DISP * tile_rows * lax.axis_size("row") * tile_cols * lax.axis_size("col")
    weight_grad = lax.psum(local_grad, ("row", "col")) / math.sqrt(total_cells)
    left_accum = jnp.zeros((tile_rows, tile_cols, channels), jnp.float32)
    grad_band = jnp.zeros((tile_rows, band_width, channels), jnp.float32)
    for disp_index in range(DISP):
        band_start = band_base - STEP * disp_index
        shifted = right_band[:, band_start : band_start + tile_cols].astype(jnp.float32)
        spread = jnp.einsum(
            "hwg,cg->hwc",
            grad_volume[disp_index].astype(jnp.float32),
            group_table,
            precision=lax.Precision.HIGHEST,
        )
        left_accum = left_accum + spread * shifted
        contrib = spread * left_float
        grad_band = grad_band + jnp.pad(
            contrib, ((0, 0), (band_start, band_width - band_start - tile_cols), (0, 0))
        )

    def band_piece(hop_index):
        return grad_band[
            :, band_base - hop_index * tile_cols : band_base - (hop_index - 1) * tile_cols
        ]

    right_accum = band_piece(hop_count)
    for hop_index in range(hop_count - 1, -1, -1):
        right_accum = shifted_2(right_accum, "col", -1) + band_piece(hop_index)
    left_grad = (left_accum / group_size).astype(jnp.bfloat16)
    right_grad = (right_accum / group_size).astype(jnp.bfloat16)
    return (output, weight_grad, left_grad, right_grad)


def solution(mesh):
    in_specs = (P("row", "col", None), P("row", "col", None), P(), P(None, "row", "col", None))
    out_specs = (P(None, "row", "col", None), P(), P("row", "col", None), P("row", "col", None))
    return jax.shard_map(
        on_device, mesh=mesh, in_specs=in_specs, out_specs=out_specs, check_vma=False
    )
```

profile of v0, /device:TPU:1, one launch (start us, length us, event | category | flops | bytes accessed | tf_op | source)
XLA Modules:
  0.0 492.1 jit_solution(12546032081893617520)
XLA Ops:
  7.2 2.0 copy.212
  9.3 4.1 collective-permute-start.6
  14.7 5.7 %collective-permute-start = (bf16[4,64,320]{2,1,0:T(8,128)(2,1)S(1)}, bf16[4,64,320]{2,1,0:T(8,128)(2,1)}, u32[]{:S(2)}, u32[]{:S(2)}) collective-permute-start(bf16[4,64,320]{2,1,0:T(8,128)(2,1)S(1)} %copy-done.27), channel_id=1, source_target_pairs={{0,1},{1,2},{2,3},{3,4},{4,5},{5,6},{6,7},{7,8},{8,9},{9,10},{10,1... | collective-permute-start | bytes 491528 | tf_op jit(solution)/shard_map/ppermute | solution.py:19
  21.2 3.8 collective-permute-done.7
  25.8 6.6 %collective-permute-start.8 = (bf16[24,6,1,32]{3,0,2,1:T(8,128)(2,1)S(1)}, bf16[24,6,1,32]{3,0,2,1:T(8,128)(2,1)S(1)}, u32[]{:S(2)}, u32[]{:S(2)}) collective-permute-start(bf16[24,6,1,32]{3,0,2,1:T(8,128)(2,1)S(1)} %get-tuple-element.20), channel_id=1, source_target_pairs={{0,1},{1,2},{2,3},{3,4},{4,5},{5,6},{6,7},{7,8},{8,9},{9,10},{10,1... | collective-permute-start | bytes 27656 | tf_op jit(solution)/shard_map/ppermute | solution.py:30
  32.3 1.9 collective-permute-start.9
  35.4 5.1 %copy.211 = bf16[1,24,4,64,32]{4,0,3,2,1:T(2,128)(2,1)} copy(bf16[1,24,4,64,32]{3,4,2,1,0:T(8,128)(2,1)S(1)} %bitcast.279) | data formatting | bytes 786432 | tf_op jit(solution)/shard_map/broadcast_in_dim | solution.py:86
  40.5 2.5 maximum_bitcast_fusion
  44.3 5.4 %select_convert_fusion = bf16[24,4,8,9,40]{4,2,3,1,0:T(8,128)(2,1)S(1)} fusion(pred[8,9]{0,1:T(8,128)(4,1)S(1)} %copy-done.29, bf16[3,3,3,40,32]{3,4,2,1,0:T(8,128)(2,1)S(1)} %copy-done, bf16[24,6,1,7,2,32]{5,3,4,1,0,2:T(8,128)(2,1)S(1)} %slice.377, bf16[24,6,1,8,9,32]{5,3,4,1,0,2:T(8,128)(2,1)S(1)} %copy.216), kind=kOutput, calls=%fused_computation.52 | convolution fusion | flops 467472384 | bytes 1414728 | tf_op jit(solution)/shard_map/conv_general_dilated | solution.py:40
  99.1 6.1 %convert_multiply_fusion.23 = (f32[4,64,320]{2,1,0:T(8,128)}, f32[4,64,320]{2,1,0:T(8,128)}, f32[4,64,320]{2,1,0:T(8,128)}, f32[4,64,320]{2,1,0:T(8,128)}, f32[4...) fusion(bf16[4,64,320]{2,1,0:T(8,128)(2,1)S(1)} %copy-done.1, ...), kind=kOutput, calls=%fused_computation.27 | convolution fusion | flops 8122880 | bytes 11982080 | tf_op jit(solution)/shard_map/hwg,cg->hwc/dot_general | solution.py:100
  105.5 5.7 %collective-permute-start.1 = (bf16[4,64,320]{2,1,0:T(8,128)(2,1)}, bf16[4,64,320]{2,1,0:T(8,128)(2,1)S(1)}, u32[]{:S(2)}, u32[]{:S(2)}) collective-permute-start(bf16[4,64,320]{2,1,0:T(8,128)(2,1)} %collective-permute-done), channel_id=1, source_target_pairs={{0,1},{1,2},{2,3},{3,4},{4,5},{5,6},{6,7},{7,8},{8,9},{9,10},{10,1... | collective-permute-start | bytes 491528 | tf_op jit(solution)/shard_map/ppermute | solution.py:19
  111.4 2.3 collective-permute-done.1
  127.9 3.4 collective-permute-start.2
  132.8 3.0 multiply_convert_fusion.1
  138.6 1.8 fusion.250
  140.4 2.3 copy.202
  142.7 7.6 %collective-permute-start.4 = (bf16[24,6,1,40]{3,0,2,1:T(8,128)(2,1)S(1)}, bf16[24,6,1,40]{3,0,2,1:T(8,128)(2,1)S(1)}, u32[]{:S(2)}, u32[]{:S(2)}) collective-permute-start(bf16[24,6,1,40]{3,0,2,1:T(8,128)(2,1)S(1)} %copy.202), channel_id=1, source_target_pairs={{0,1},{1,2},{2,3},{3,4},{4,5},{5,6},{6,7},{7,8},{8,9},{9,10},{10,1... | collective-permute-start | bytes 34568 | tf_op jit(solution)/shard_map/ppermute | solution.py:30
  151.3 1.9 collective-permute-start.5
  153.2 4.3 pad_add_fusion
  158.3 1.9 collective-permute-start.10
  161.3 2.1 copy.205
  163.4 2.7 pad_maximum_fusion.1
  167.6 12.4 %copy.210 = bf16[1,26,6,66,40]{4,0,3,2,1:T(2,128)(2,1)} copy(bf16[1,26,6,66,40]{3,4,2,1,0:T(8,128)(2,1)} %pad_bitcast_fusion) | data formatting | bytes 1647360 | tf_op jit(solution)/shard_map/broadcast_in_dim | solution.py:85
  180.0 42.7 %fusion.252 = f32[3,3,3,40,32]{3,4,2,1,0:T(8,128)} fusion(bf16[1,26,6,66,40]{4,0,3,2,1:T(2,128)(2,1)} %copy.210, bf16[1,24,4,64,32]{4,0,3,2,1:T(2,128)(2,1)} %copy.211), kind=kOutput, calls=%fused_computation.321 | convolution fusion | flops 424673280 | bytes 1355136 | tf_op jit(solution)/shard_map/transpose | solution.py:92
  222.7 3.9 fusion.257
  226.6 3.3 copy.290
  230.9 6.0 %select_convert_fusion.1 = bf16[24,4,8,9,32]{4,2,3,1,0:T(8,128)(2,1)S(1)} fusion(pred[8,9]{0,1:T(8,128)(4,1)S(1)} %copy-done.29, bf16[3,3,3,40,32]{3,4,2,1,0:T(8,128)(2,1)S(1)} %copy-done, bf16[24,6,1,7,2,40]{5,3,4,1,0,2:T(8,128)(2,1)S(1)} %slice.373, bf16[24,6,1,8,9,40]{5,3,4,1,0,2:T(8,128)(2,1)S(1)} %copy.208), kind=kOutput, calls=%fused_computation.53 | convolution fusion | flops 467970048 | bytes 1502280 | tf_op jit(solution)/shard_map/conv_general_dilated | solution.py:40
  238.1 1.8 slice_add_fusion.1
  240.0 1.9 collective-permute-start.11
  243.8 237.6 %all-reduce.27.cloned.1.call-done = f32[3,3,3,40,32]{3,4,2,1,0:T(8,128)} async-done(((f32[3,3,3,40,32]{3,4,2,1,0:T(8,128)}), f32[3,3,3,40,32]{3,4,2,1,0:T(8,128)}) %all-reduce.27.cloned.1.call-update) | async-done | bytes 138256 | tf_op jit(solution)/shard_map/psum | solution.py:94
  481.5 1.8 broadcast_multiply_fusion
  483.3 1.8 fusion.70
  (217 shorter events, 81.3 us)
Async XLA Ops:
  7.2 36.9 %copy-start = (bf16[3,3,3,40,32]{3,4,2,1,0:T(8,128)(2,1)S(1)}, bf16[3,3,3,40,32]{3,4,2,1,0:T(8,128)(2,1)}, u32[]{:S(2)}) copy-start(bf16[3,3,3,40,32]{3,4,2,1,0:T(8,128)(2,1)} %param.6) | copy-start | bytes 207364
  7.2 7.6 %copy-start.27 = (bf16[4,64,320]{2,1,0:T(8,128)(2,1)S(1)}, bf16[4,64,320]{2,1,0:T(8,128)(2,1)}, u32[]{:S(2)}) copy-start(bf16[4,64,320]{2,1,0:T(8,128)(2,1)} %param.5) | copy-start | bytes 491524
  7.2 474.3 %all-reduce.27.cloned.1.call-start = ((), (), s32[]{:S(2)}) async-start(), calls=%async_computation | async-start | bytes 884736 | tf_op jit(solution)/shard_map/psum | solution.py:94
  9.2 25.1 %copy-start.1 = (bf16[4,64,320]{2,1,0:T(8,128)(2,1)S(1)}, bf16[4,64,320]{2,1,0:T(8,128)(2,1)}, u32[]{:S(2)}) copy-start(bf16[4,64,320]{2,1,0:T(8,128)(2,1)} %param.4) | copy-start | bytes 491524
  9.2 26.2 %copy-start.4 = (bf16[24,4,64,32]{2,3,1,0:T(8,128)(2,1)S(1)}, bf16[24,4,64,32]{2,3,1,0:T(8,128)(2,1)}, u32[]{:S(2)}) copy-start(bf16[24,4,64,32]{2,3,1,0:T(8,128)(2,1)} %param.7) | copy-start | bytes 1179652
  9.3 11.8 %collective-permute-start.6 = (bf16[24,1,64,32]{3,0,2,1:T(8,128)(2,1)S(1)}, bf16[24,1,64,32]{3,0,2,1:T(8,128)(2,1)S(1)}, u32[]{:S(2)}, u32[]{:S(2)}) collective-permute-start(bf16[24,1,64,32]{3,0,2,1:T(8,128)(2,1)S(1)} %get-tuple-element.46), channel_id=1, source_target_pairs={{0,32},{32,64},{64,96},{96,128},{128,160},{160,192},{192,224},{1,3... | collective-permute-start | bytes 294920 | tf_op jit(solution)/shard_map/ppermute | solution.py:30
  13.4 11.6 %collective-permute-start.7 = (bf16[24,1,64,32]{3,0,2,1:T(8,128)(2,1)S(1)}, bf16[24,1,64,32]{3,0,2,1:T(8,128)(2,1)S(1)}, u32[]{:S(2)}, u32[]{:S(2)}) collective-permute-start(bf16[24,1,64,32]{3,0,2,1:T(8,128)(2,1)S(1)} %get-tuple-element.47), channel_id=1, source_target_pairs={{32,0},{64,32},{96,64},{128,96},{160,128},{192,160},{224,192},{33,... | collective-permute-start | bytes 294920 | tf_op jit(solution)/shard_map/ppermute | solution.py:32
  14.7 90.8 %collective-permute-start = (bf16[4,64,320]{2,1,0:T(8,128)(2,1)S(1)}, bf16[4,64,320]{2,1,0:T(8,128)(2,1)}, u32[]{:S(2)}, u32[]{:S(2)}) collective-permute-start(bf16[4,64,320]{2,1,0:T(8,128)(2,1)S(1)} %copy-done.27), channel_id=1, source_target_pairs={{0,1},{1,2},{2,3},{3,4},{4,5},{5,6},{6,7},{7,8},{8,9},{9,10},{10,1... | collective-permute-start | bytes 491528 | tf_op jit(solution)/shard_map/ppermute | solution.py:19
  25.8 14.8 %collective-permute-start.8 = (bf16[24,6,1,32]{3,0,2,1:T(8,128)(2,1)S(1)}, bf16[24,6,1,32]{3,0,2,1:T(8,128)(2,1)S(1)}, u32[]{:S(2)}, u32[]{:S(2)}) collective-permute-start(bf16[24,6,1,32]{3,0,2,1:T(8,128)(2,1)S(1)} %get-tuple-element.20), channel_id=1, source_target_pairs={{0,1},{1,2},{2,3},{3,4},{4,5},{5,6},{6,7},{7,8},{8,9},{9,10},{10,1... | collective-permute-start | bytes 27656 | tf_op jit(solution)/shard_map/ppermute | solution.py:30
  32.3 8.2 %collective-permute-start.9 = (bf16[24,6,1,32]{3,0,2,1:T(8,128)(2,1)S(1)}, bf16[24,6,1,32]{3,0,2,1:T(8,128)(2,1)S(1)}, u32[]{:S(2)}, u32[]{:S(2)}) collective-permute-start(bf16[24,6,1,32]{3,0,2,1:T(8,128)(2,1)S(1)} %get-tuple-element.21), channel_id=1, source_target_pairs={{1,0},{2,1},{3,2},{4,3},{5,4},{6,5},{7,6},{8,7},{9,8},{10,9},{11,1... | collective-permute-start | bytes 27656 | tf_op jit(solution)/shard_map/ppermute | solution.py:32
  52.9 46.2 %copy-start.6 = (f32[4,64,320]{2,1,0:T(8,128)}, f32[4,64,320]{2,1,0:T(8,128)S(1)}, u32[]{:S(2)}) copy-start(f32[4,64,320]{2,1,0:T(8,128)S(1)} %fusion.112) | copy-start | bytes 983044
  53.3 45.8 %copy-start.8 = (f32[4,64,320]{2,1,0:T(8,128)}, f32[4,64,320]{2,1,0:T(8,128)S(1)}, u32[]{:S(2)}) copy-start(f32[4,64,320]{2,1,0:T(8,128)S(1)} %fusion.114) | copy-start | bytes 983044
  53.8 45.3 %copy-start.10 = (f32[4,64,320]{2,1,0:T(8,128)}, f32[4,64,320]{2,1,0:T(8,128)S(1)}, u32[]{:S(2)}) copy-start(f32[4,64,320]{2,1,0:T(8,128)S(1)} %fusion.116) | copy-start | bytes 983044
  105.2 9.5 %copy-start.5 = (f32[24,4,64,40]{2,3,1,0:T(8,128)S(1)}, f32[24,4,64,40]{2,3,1,0:T(8,128)}, u32[]{:S(2)}) copy-start(f32[24,4,64,40]{2,3,1,0:T(8,128)} %fusion.45) | copy-start | bytes 2949124
  105.5 8.2 %collective-permute-start.1 = (bf16[4,64,320]{2,1,0:T(8,128)(2,1)}, bf16[4,64,320]{2,1,0:T(8,128)(2,1)S(1)}, u32[]{:S(2)}, u32[]{:S(2)}) collective-permute-start(bf16[4,64,320]{2,1,0:T(8,128)(2,1)} %collective-permute-done), channel_id=1, source_target_pairs={{0,1},{1,2},{2,3},{3,4},{4,5},{5,6},{6,7},{7,8},{8,9},{9,10},{10,1... | collective-permute-start | bytes 491528 | tf_op jit(solution)/shard_map/ppermute | solution.py:19
  124.4 8.2 %copy-start.28 = (bf16[4,64,320]{2,1,0:T(8,128)(2,1)S(1)}, bf16[4,64,320]{2,1,0:T(8,128)(2,1)}, u32[]{:S(2)}) copy-start(bf16[4,64,320]{2,1,0:T(8,128)(2,1)} %param.5) | copy-start | bytes 491524
  124.9 7.7 %copy-start.26 = (f32[4,64,320]{2,1,0:T(8,128)S(1)}, f32[4,64,320]{2,1,0:T(8,128)}, u32[]{:S(2)}) copy-start(f32[4,64,320]{2,1,0:T(8,128)} %fusion.104) | copy-start | bytes 983044
  125.5 7.1 %copy-start.25 = (f32[4,64,320]{2,1,0:T(8,128)S(1)}, f32[4,64,320]{2,1,0:T(8,128)}, u32[]{:S(2)}) copy-start(f32[4,64,320]{2,1,0:T(8,128)} %fusion.102) | copy-start | bytes 983044
  126.0 6.6 %copy-start.22 = (f32[4,64,320]{2,1,0:T(8,128)S(1)}, f32[4,64,320]{2,1,0:T(8,128)}, u32[]{:S(2)}) copy-start(f32[4,64,320]{2,1,0:T(8,128)} %fusion.138) | copy-start | bytes 983044
  126.0 6.6 %copy-start.24 = (f32[4,64,320]{2,1,0:T(8,128)S(1)}, f32[4,64,320]{2,1,0:T(8,128)}, u32[]{:S(2)}) copy-start(f32[4,64,320]{2,1,0:T(8,128)} %fusion.100) | copy-start | bytes 983044
  126.5 6.1 %copy-start.21 = (f32[4,64,320]{2,1,0:T(8,128)S(1)}, f32[4,64,320]{2,1,0:T(8,128)}, u32[]{:S(2)}) copy-start(f32[4,64,320]{2,1,0:T(8,128)} %fusion.136) | copy-start | bytes 983044
  127.1 5.6 %copy-start.19 = (f32[4,64,320]{2,1,0:T(8,128)S(1)}, f32[4,64,320]{2,1,0:T(8,128)}, u32[]{:S(2)}) copy-start(f32[4,64,320]{2,1,0:T(8,128)} %fusion.132) | copy-start | bytes 983044
  127.1 5.6 %copy-start.20 = (f32[4,64,320]{2,1,0:T(8,128)S(1)}, f32[4,64,320]{2,1,0:T(8,128)}, u32[]{:S(2)}) copy-start(f32[4,64,320]{2,1,0:T(8,128)} %fusion.134) | copy-start | bytes 983044
  127.6 5.1 %copy-start.7 = (f32[4,64,320]{2,1,0:T(8,128)S(1)}, f32[4,64,320]{2,1,0:T(8,128)}, u32[]{:S(2)}) copy-start(f32[4,64,320]{2,1,0:T(8,128)} %copy-done.6) | copy-start | bytes 983044
  127.6 5.1 %copy-start.9 = (f32[4,64,320]{2,1,0:T(8,128)S(1)}, f32[4,64,320]{2,1,0:T(8,128)}, u32[]{:S(2)}) copy-start(f32[4,64,320]{2,1,0:T(8,128)} %copy-done.8) | copy-start | bytes 983044
  127.6 5.1 %copy-start.11 = (f32[4,64,320]{2,1,0:T(8,128)S(1)}, f32[4,64,320]{2,1,0:T(8,128)}, u32[]{:S(2)}) copy-start(f32[4,64,320]{2,1,0:T(8,128)} %copy-done.10) | copy-start | bytes 983044
  127.9 9.3 %collective-permute-start.2 = (bf16[24,1,64,40]{2,3,1,0:T(8,128)(2,1)S(1)}, bf16[24,1,64,40]{2,3,1,0:T(8,128)(2,1)S(1)}, u32[]{:S(2)}, u32[]{:S(2)}) collective-permute-start(bf16[24,1,64,40]{2,3,1,0:T(8,128)(2,1)S(1)} %get-tuple-element.50), channel_id=1, source_target_pairs={{0,32},{32,64},{64,96},{96,128},{128,160},{160,192},{192,224},{1,3... | collective-permute-start | bytes 368648 | tf_op jit(solution)/shard_map/ppermute | solution.py:30
  131.3 6.9 %collective-permute-start.3 = (bf16[24,1,64,40]{2,3,1,0:T(8,128)(2,1)S(1)}, bf16[24,1,64,40]{2,3,1,0:T(8,128)(2,1)S(1)}, u32[]{:S(2)}, u32[]{:S(2)}) collective-permute-start(bf16[24,1,64,40]{2,3,1,0:T(8,128)(2,1)S(1)} %get-tuple-element.51), channel_id=1, source_target_pairs={{32,0},{64,32},{96,64},{128,96},{160,128},{192,160},{224,192},{33,... | collective-permute-start | bytes 368648 | tf_op jit(solution)/shard_map/ppermute | solution.py:32
  142.7 17.6 %collective-permute-start.4 = (bf16[24,6,1,40]{3,0,2,1:T(8,128)(2,1)S(1)}, bf16[24,6,1,40]{3,0,2,1:T(8,128)(2,1)S(1)}, u32[]{:S(2)}, u32[]{:S(2)}) collective-permute-start(bf16[24,6,1,40]{3,0,2,1:T(8,128)(2,1)S(1)} %copy.202), channel_id=1, source_target_pairs={{0,1},{1,2},{2,3},{3,4},{4,5},{5,6},{6,7},{7,8},{8,9},{9,10},{10,1... | collective-permute-start | bytes 34568 | tf_op jit(solution)/shard_map/ppermute | solution.py:30
  151.3 10.0 %collective-permute-start.5 = (bf16[24,6,1,40]{3,0,2,1:T(8,128)(2,1)S(1)}, bf16[24,6,1,40]{3,0,2,1:T(8,128)(2,1)S(1)}, u32[]{:S(2)}, u32[]{:S(2)}) collective-permute-start(bf16[24,6,1,40]{3,0,2,1:T(8,128)(2,1)S(1)} %copy.203), channel_id=1, source_target_pairs={{1,0},{2,1},{3,2},{4,3},{5,4},{6,5},{7,6},{8,7},{9,8},{10,9},{11,1... | collective-permute-start | bytes 34568 | tf_op jit(solution)/shard_map/ppermute | solution.py:32
  158.3 79.3 %collective-permute-start.10 = (f32[4,64,320]{2,1,0:T(8,128)}, f32[4,64,320]{2,1,0:T(8,128)}, u32[]{:S(2)}, u32[]{:S(2)}) collective-permute-start(f32[4,64,320]{2,1,0:T(8,128)} %slice.426), channel_id=1, source_target_pairs={{1,0},{2,1},{3,2},{4,3},{5,4},{6,5},{7,6},{8,7},{9,8},{10,9},{11,1... | collective-permute-start | bytes 983048 | tf_op jit(solution)/shard_map/ppermute | solution.py:19
  240.0 243.3 %collective-permute-start.11 = (f32[4,64,320]{2,1,0:T(8,128)}, f32[4,64,320]{2,1,0:T(8,128)}, u32[]{:S(2)}, u32[]{:S(2)}) collective-permute-start(f32[4,64,320]{2,1,0:T(8,128)} %slice_add_fusion.1), channel_id=1, source_target_pairs={{1,0},{2,1},{3,2},{4,3},{5,4},{6,5},{7,6},{8,7},{9,8},{10,9},{11,1... | collective-permute-start | bytes 983048 | tf_op jit(solution)/shard_map/ppermute | solution.py:19
  (11 other events, 41.1 us)
Sparse Core Ops, SparseCore 0:
  222.9 258.5 all-reduce.26
where the time goes:
time: 497 us; the launch traced here: 492 us
  waiting for transfers between devices  245 us (49%)
  matrix products  93 us (19%)
  local copies, waits for them, and re-layouts  74 us (15%)
  starting transfers between devices  43.3 us (9%)
  other arithmetic  20.8 us (4%)
  between operations  15.6 us (3%)
    psum x1, waiting for transfers between devices, on_device(): weight_grad = lax.psum(local_grad, ('row', 'col')) / math.sqrt(total_cells)  238 us
    transpose x1, matrix products, on_device(): local_grad = jnp.transpose(kernel_raw, (1, 2, 3, 0, 4))  42.7 us
    dot_general x24, matrix products, on_device(): jnp.einsum('hwg,cg->hwc', grad_volume[disp_index].astype(jnp.float32), gr...  25.2 us
    ppermute x4, starting transfers between devices, with_halo(): lax.ppermute(tail, axis, [(i, (i + 1) % count) for i in range(ends)])  21.7 us
    convert_element_type x50, local copies, waits for them, and re-layouts, on_device(): grad_volume = conv_valid(padded_cotangent, flipped).astype(jnp.bfloat16)  21.1 us
    unnamed x88, local copies, waits for them, and re-layouts  20.9 us
    ppermute x4, starting transfers between devices, shifted_2(): return lax.ppermute(block, axis, route)  15.2 us
    broadcast_in_dim x2, local copies, waits for them, and re-layouts, on_device(): full_pad[None]  13.9 us
  transfers between devices with their start and end apart: 13, of which 5 were waited for; matrix products, arithmetic and copies ran while one was open for 33% of the time, Pallas kernels for 0%

commit v1 on v0

v1 whole, which is shorter than its diff:
```python
import functools
import math

import jax
import jax.numpy as jnp
from jax import lax
from jax.experimental import pallas as pl
from jax.experimental.pallas import tpu as pltpu
from jax.sharding import PartitionSpec as P

DISP = 24
STEP = 4
OUT_D = 6
IN_D = OUT_D + 2
WINDOWS = DISP // OUT_D
LANES = 256
BF = jnp.bfloat16
F32 = jnp.float32
MESH = pl.DeviceIdType.MESH
NEIGHBOURS = [(dr, dc) for dr in (-1, 0, 1) for dc in (-1, 0, 1) if (dr, dc) != (0, 0)]


def dot(a, b, contract=((1,), (0,))):
    return lax.dot_general(a, b, (contract, ((), ())), preferred_element_type=F32)


def iota(shape, dim):
    return lax.broadcasted_iota(jnp.int32, shape, dim)


def kernel(
    nrow, ncol, chunk, owners, scale,
    l_ref, r_ref, w_ref, c_ref,
    cost_ref, wg_ref, lg_ref, rg_ref,
    rband, rf0, rf4, lf, sel, band_n, band_t, cs, vs, vt, edge_c, edge_v, halo_c, halo_v,
    gv, spread, racc0, racc4, back_send, back_recv, dsum, slots1, part2, slots2, full, obuf,
    sem_rs, sem_rr, sem_cs, sem_cr, sem_vs, sem_vr, sem_bs, sem_br,
    sem1_s, sem1_r, sem2_s, sem2_r, sem3_s, sem3_r,
):
    rows, cols, channels = l_ref.shape
    groups, feats = w_ref.shape[3], w_ref.shape[4]
    group_size = channels // groups
    cells = rows * cols
    row, col = lax.axis_index("row"), lax.axis_index("col")

    def at(dr, dc):
        return (lax.rem(row + dr + nrow, nrow), lax.rem(col + dc + ncol, ncol))

    barrier = pltpu.get_barrier_semaphore()

    def hello_col(step, carry):
        pl.semaphore_signal(barrier, inc=1, device_id=at(0, step), device_id_type=MESH)
        return carry

    def hello_row(step, carry):
        pl.semaphore_signal(barrier, inc=1, device_id=at(step, 0), device_id_type=MESH)
        return carry

    lax.fori_loop(1, ncol, hello_col, 0)
    lax.fori_loop(1, nrow, hello_row, 0)
    for dr, dc in NEIGHBOURS:
        if dr != 0 and dc != 0:
            pl.semaphore_signal(barrier, inc=1, device_id=at(dr, dc), device_id_type=MESH)
    pl.semaphore_wait(barrier, ncol - 1 + nrow - 1 + 4)

    def copy(src, dst, send, recv, target):
        return pltpu.make_async_remote_copy(
            src_ref=src, dst_ref=dst, send_sem=send, recv_sem=recv,
            device_id=target, device_id_type=MESH,
        )

    right_copies = [
        copy(r_ref, rband.at[:, 32:96], sem_rs.at[0], sem_rr.at[0], at(0, 1)),
        copy(r_ref.at[:, cols - 32 : cols], rband.at[:, 0:32], sem_rs.at[1], sem_rr.at[1], at(0, 2)),
    ]
    for c in right_copies:
        c.start()

    def halo_copies(body, edge, halo, send, recv):
        out = []
        for n, (dr, dc) in enumerate(NEIGHBOURS):
            if dc == 0:
                src = body.at[1, :, rows if dr == 1 else 1]
                dst = body.at[1, :, 0 if dr == 1 else rows + 1]
            else:
                src = edge.at[1 if dc == 1 else 0]
                dst = halo.at[0 if dc == 1 else 1, 1 - dr]
            out.append(copy(src, dst, send.at[n], recv.at[n], at(dr, dc)))
        return out

    def edge_pieces(body):
        first, last = [], []
        for k in range(WINDOWS):
            for h in range(rows):
                first.append(body[1, k, 1 + h, 0:16].astype(F32)[0:1])
                last.append(body[1, k, 1 + h, cols - 16 : cols].astype(F32)[15:16])
        return first, last

    def fill_edges(edge, body):
        for side, lines in enumerate(edge_pieces(body)):
            acc = jnp.zeros((16, LANES), F32)
            for n, line in enumerate(lines):
                acc = jnp.where(iota((16, LANES), 0) == n, line, acc)
            edge[side] = acc.astype(BF)

    def clear_outside(body, halo):
        for cond, u, h in ((row == 0, 0, 0), (row == nrow - 1, 2, rows + 1)):
            @pl.when(cond)
            def _():
                for k in range(WINDOWS):
                    body[1, k, h] = jnp.zeros((cols, LANES), BF)
                for side in range(2):
                    halo[side, u] = jnp.zeros((16, LANES), BF)
        for cond, side in ((col == 0, 0), (col == ncol - 1, 1)):
            @pl.when(cond)
            def _():
                for u in range(3):
                    halo[side, u] = jnp.zeros((16, LANES), BF)

    def write_shifts(body, halo):
        lines = [[halo[side, u].astype(F32) for u in range(3)] for side in range(2)]
        where = iota((cols, LANES), 0)
        for k in range(WINDOWS):
            for h in range(rows + 2):
                u, n = (0, rows - 1) if h == 0 else ((2, 0) if h == rows + 1 else (1, h - 1))
                n = n + rows * k
                mid = body[1, k, h].astype(F32)
                before = jnp.where(where == 0, lines[0][u][n : n + 1], pltpu.roll(mid, 1, 0))
                after = jnp.where(where == cols - 1, lines[1][u][n : n + 1], pltpu.roll(mid, cols - 1, 0))
                body[0, k, h] = before.astype(BF)
                body[2, k, h] = after.astype(BF)

    for k in range(WINDOWS):
        parts = []
        for j in range(IN_D):
            d = OUT_D * k - 1 + j
            if 0 <= d < DISP:
                parts.append(c_ref[d].reshape(cells, feats))
            else:
                parts.append(jnp.zeros((cells, feats), BF))
        cs[1, k, 1 : rows + 1] = jnp.concatenate(parts, axis=1).reshape(rows, cols, LANES)
    fill_edges(edge_c, cs)
    cot_copies = halo_copies(cs, edge_c, halo_c, sem_cs, sem_cr)
    for c in cot_copies:
        c.start()

    lf[...] = l_ref[...].astype(F32)
    for i in range(OUT_D):
        r = iota((channels, LANES), 0) + i * channels
        sel[i] = jnp.where(r // group_size == iota((channels, LANES), 1), 1.0, 0.0).astype(BF)
    f_idx = iota((feats, OUT_D * LANES), 0)
    lane = iota((feats, OUT_D * LANES), 1)
    banded = jnp.zeros((9 * groups, OUT_D * LANES), F32)
    for a in range(3):
        tap = jnp.where(
            (lane % feats == f_idx) & (lane // LANES - (lane % LANES) // feats + 2 == a), 1.0, 0.0
        ).astype(BF)
        wa = w_ref[a].astype(F32).reshape(9 * groups, feats).astype(BF)
        banded = banded + dot(wa, tap)
    for n in range(9):
        tall = [banded[groups * n : groups * (n + 1), LANES * i : LANES * (i + 1)] for i in range(OUT_D)]
        tall.append(jnp.zeros((LANES - OUT_D * groups, LANES), F32))
        tall = jnp.concatenate(tall, axis=0)
        band_n[LANES * n : LANES * (n + 1)] = tall.astype(BF)
        band_t[LANES * n : LANES * (n + 1)] = tall.T.astype(BF)

    for c in right_copies:
        c.wait_recv()
    @pl.when(col < 1)
    def _():
        rband[:, 32:96] = jnp.zeros((rows, 64, channels), BF)

    @pl.when(col < 2)
    def _():
        rband[:, 0:32] = jnp.zeros((rows, 32, channels), BF)

    for h in range(rows):
        rf0[h, 0:96] = rband[h].astype(F32)
        rf0[h, 96:160] = r_ref[h].astype(F32)
        rf4[h, 0:152] = rf0[h, 4:156]
        rf4[h, 152:160] = rf0[h, 152:160]

    def shifted(k, i, h=None):
        start = pl.multiple_of(96 - STEP * (OUT_D * k + i) - (STEP if i % 2 else 0), 8)
        src = rf4 if i % 2 else rf0
        if h is None:
            return src[:, pl.ds(start, cols)]
        return src[h, pl.ds(start, cols)]

    def volume(k, carry):
        acc = jnp.zeros((cells, LANES), F32)
        for i in range(OUT_D):
            product = (lf[...] * shifted(k, i)).astype(BF).reshape(cells, channels)
            acc = acc + dot(product, sel[i])
        acc = (acc * (1.0 / group_size)).astype(BF)
        vs[1, k, 1 : rows + 1] = acc.reshape(rows, cols, LANES)
        vt[k] = acc.T
        return carry

    lax.fori_loop(0, WINDOWS, volume, 0)
    fill_edges(edge_v, vs)
    vol_copies = halo_copies(vs, edge_v, halo_v, sem_vs, sem_vr)
    for c in vol_copies:
        c.start()

    for c in cot_copies:
        c.wait_recv()
    clear_outside(cs, halo_c)
    write_shifts(cs, halo_c)

    dsum[9 * groups :] = jnp.zeros((dsum.shape[0] - 9 * groups, 128), F32)

    def kernel_grad(n, carry):
        t, hb = 2 - n % 3, 2 - n // 3
        acc = jnp.zeros((LANES, LANES), F32)
        for k in range(WINDOWS):
            acc = acc + dot(vt[k], cs[t, k, pl.ds(hb, rows)].reshape(cells, LANES))
        total = acc[0:groups]
        for i in range(1, OUT_D):
            total = total + pltpu.roll(acc[groups * i : groups * (i + 1)], LANES - feats * i, 1)
        dsum[pl.ds(pl.multiple_of(n * groups, 8), groups)] = total[:, 0:128]
        return carry

    lax.fori_loop(0, 9, kernel_grad, 0)

    own_rows = pl.ds(pl.multiple_of(col * chunk, 8), chunk)

    def send1(step, carry):
        r, c = at(0, step)

        @pl.when(c < owners)
        def _():
            copy(
                dsum.at[pl.ds(pl.multiple_of(c * chunk, 8), chunk)], slots1.at[col],
                sem1_s.at[step], sem1_r.at[col], (r, c),
            ).start()
        return carry

    lax.fori_loop(1, ncol, send1, 0)

    def grad_volume(k, carry):
        taps = []
        for b in range(3):
            for e in range(3):
                taps.append(cs[2 - e, k, 2 - b : 2 - b + rows].reshape(cells, LANES))
        gv[k] = dot(jnp.concatenate(taps, axis=1), band_t[...]).astype(BF)
        return carry

    lax.fori_loop(0, WINDOWS, grad_volume, 0)

    @pl.when(col < owners)
    def _():
        slots1[col] = dsum[own_rows]

        def wait1(step, carry):
            _, c = at(0, step)
            copy(slots1.at[c], slots1.at[c], sem1_s.at[step], sem1_r.at[c], at(0, step)).wait_recv()
            return carry

        lax.fori_loop(1, ncol, wait1, 0)
        total = slots1[0]
        for q in range(1, ncol):
            total = total + slots1[q]
        part2[...] = total
        slots2[row] = total

        def send2(step, carry):
            copy(part2, slots2.at[row], sem2_s.at[step], sem2_r.at[row], at(step, 0)).start()
            return carry

        lax.fori_loop(1, nrow, send2, 0)

    racc0[...] = jnp.zeros_like(racc0)
    racc4[...] = jnp.zeros_like(racc4)
    lacc = spread.at[0]
    lacc[...] = jnp.zeros((cells, channels), F32)

    def feature_grads(k, carry):
        for i in range(OUT_D):
            spread[1] = dot(gv[k], sel[i], ((1,), (1,)))
            start = pl.multiple_of(96 - STEP * (OUT_D * k + i) - (STEP if i % 2 else 0), 8)
            acc = racc4 if i % 2 else racc0
            for h in range(rows):
                s = spread[1, cols * h : cols * (h + 1)]
                lacc[cols * h : cols * (h + 1)] += s * shifted(k, i, h)
                acc[h, pl.ds(start, cols)] += s * lf[h]
        return carry

    lax.fori_loop(0, WINDOWS, feature_grads, 0)
    inv = 1.0 / group_size
    lg_ref[...] = (lacc[...] * inv).reshape(rows, cols, channels).astype(BF)
    for h in range(rows):
        racc0[h, 4:156] += racc4[h, 0:152]
        back_send[h] = racc0[h, 0:96].astype(BF)
    back_copies = [
        copy(back_send.at[:, 32:96], back_recv.at[:, 0:64], sem_bs.at[0], sem_br.at[0], at(0, -1)),
        copy(back_send.at[:, 0:32], back_recv.at[:, 64:96], sem_bs.at[1], sem_br.at[1], at(0, -2)),
    ]
    for c in back_copies:
        c.start()

    @pl.when(col < owners)
    def _():
        def wait2(step, carry):
            r, _ = at(step, 0)
            copy(part2, slots2.at[r], sem2_s.at[step], sem2_r.at[r], at(step, 0)).wait_recv()
            return carry

        lax.fori_loop(1, nrow, wait2, 0)
        total = slots2[0]
        for q in range(1, nrow):
            total = total + slots2[q]
        full[own_rows] = total * scale

        def send3(step, carry):
            copy(full.at[own_rows], full.at[own_rows], sem3_s.at[step], sem3_r.at[col], at(0, step)).start()
            return carry

        lax.fori_loop(1, ncol, send3, 0)

    for c in vol_copies:
        c.wait_recv()
    clear_outside(vs, halo_v)
    write_shifts(vs, halo_v)

    def forward(k, carry):
        taps = []
        for b in range(3):
            for e in range(3):
                taps.append(vs[e, k, b : b + rows].reshape(cells, LANES))
        obuf[k] = dot(jnp.concatenate(taps, axis=1), band_n[...])
        return carry

    lax.fori_loop(0, WINDOWS, forward, 0)
    for k in range(WINDOWS):
        for i in range(OUT_D):
            j = i + 1
            value = obuf[k, :, feats * j : feats * (j + 1)]
            if i == 0 and k > 0:
                value = value + obuf[k - 1, :, feats * (IN_D - 1) : feats * IN_D]
            if i == OUT_D - 1 and k < WINDOWS - 1:
                value = value + obuf[k + 1, :, 0:feats]
            cost_ref[OUT_D * k + i] = value.astype(BF).reshape(rows, cols, feats)

    for c in back_copies:
        c.wait_recv()
    near = jnp.where(col < ncol - 1, 1.0, 0.0).astype(F32)
    far = jnp.where(col < ncol - 2, 1.0, 0.0).astype(F32)
    for h in range(rows):
        own = racc0[h, 96:160] + near * back_recv[h, 0:64].astype(F32)
        tail = own[32:64] + far * back_recv[h, 64:96].astype(F32)
        rg_ref[h, 0:32] = (own[0:32] * inv).astype(BF)
        rg_ref[h, 32:64] = (tail * inv).astype(BF)

    def wait3(step, carry):
        _, c = at(0, step)

        @pl.when(c < owners)
        def _():
            piece = full.at[pl.ds(pl.multiple_of(c * chunk, 8), chunk)]
            copy(piece, piece, sem3_s.at[step], sem3_r.at[c], at(0, step)).wait_recv()
        return carry

    lax.fori_loop(1, ncol, wait3, 0)
    for b in range(3):
        for e in range(3):
            block = full[groups * (3 * b + e) : groups * (3 * b + e + 1)]
            for a in range(3):
                wg_ref[a, b, e] = block[:, feats * (2 - a) : feats * (3 - a)]

    for c in right_copies + cot_copies + vol_copies + back_copies:
        c.wait_send()

    def sent1(step, carry):
        _, c = at(0, step)

        @pl.when(c < owners)
        def _():
            copy(dsum.at[own_rows], slots1.at[col], sem1_s.at[step], sem1_r.at[col], at(0, step)).wait_send()
        return carry

    lax.fori_loop(1, ncol, sent1, 0)

    @pl.when(col < owners)
    def _():
        def sent2(step, carry):
            copy(part2, slots2.at[row], sem2_s.at[step], sem2_r.at[row], at(step, 0)).wait_send()
            return carry

        lax.fori_loop(1, nrow, sent2, 0)

        def sent3(step, carry):
            copy(full.at[own_rows], full.at[own_rows], sem3_s.at[step], sem3_r.at[col], at(0, step)).wait_send()
            return carry

        lax.fori_loop(1, ncol, sent3, 0)


def on_device(nrow, ncol, left, right, weight, cotangent):
    rows, cols, channels = left.shape
    groups, feats = weight.shape[3], weight.shape[4]
    cells = rows * cols
    chunk = -(-9 * groups // ncol)
    chunk = -(-chunk // 16) * 16
    owners = -(-9 * groups // chunk)
    scale = 1.0 / math.sqrt(DISP * rows * nrow * cols * ncol)
    dma = pltpu.SemaphoreType.DMA
    body = pltpu.VMEM((3, WINDOWS, rows + 2, cols, LANES), BF)
    edge = pltpu.VMEM((2, 16, LANES), BF)
    halo = pltpu.VMEM((2, 3, 16, LANES), BF)
    scratch = [
        pltpu.VMEM((rows, 96, channels), BF),
        pltpu.VMEM((rows, 160, channels), F32),
        pltpu.VMEM((rows, 160, channels), F32),
        pltpu.VMEM((rows, cols, channels), F32),
        pltpu.VMEM((OUT_D, channels, LANES), BF),
        pltpu.VMEM((9 * LANES, LANES), BF),
        pltpu.VMEM((9 * LANES, LANES), BF),
        body, body,
        pltpu.VMEM((WINDOWS, LANES, cells), BF),
        edge, edge, halo, halo,
        pltpu.VMEM((WINDOWS, cells, LANES), BF),
        pltpu.VMEM((2, cells, channels), F32),
        pltpu.VMEM((rows, 160, channels), F32),
        pltpu.VMEM((rows, 160, channels), F32),
        pltpu.VMEM((rows, 96, channels), BF),
        pltpu.VMEM((rows, 96, channels), BF),
        pltpu.VMEM((ncol * chunk, 128), F32),
        pltpu.VMEM((ncol, chunk, 128), F32),
        pltpu.VMEM((chunk, 128), F32),
        pltpu.VMEM((nrow, chunk, 128), F32),
        pltpu.VMEM((ncol * chunk, 128), F32),
        pltpu.VMEM((WINDOWS, cells, LANES), F32),
        dma((2,)), dma((2,)), dma((8,)), dma((8,)), dma((8,)), dma((8,)), dma((2,)), dma((2,)),
        dma((ncol,)), dma((ncol,)), dma((nrow,)), dma((nrow,)), dma((ncol,)), dma((ncol,)),
    ]
    vmem = pl.BlockSpec(memory_space=pltpu.VMEM)
    return pl.pallas_call(
        functools.partial(kernel, nrow, ncol, chunk, owners, scale),
        out_shape=(
            jax.ShapeDtypeStruct((DISP, rows, cols, feats), BF),
            jax.ShapeDtypeStruct(weight.shape, F32),
            jax.ShapeDtypeStruct(left.shape, BF),
            jax.ShapeDtypeStruct(right.shape, BF),
        ),
        in_specs=[vmem] * 4,
        out_specs=(vmem,) * 4,
        scratch_shapes=scratch,
        compiler_params=pltpu.CompilerParams(
            collective_id=0, has_side_effects=True, vmem_limit_bytes=56 * 1024 * 1024
        ),
        name="cost_volume",
    )(left, right, weight, cotangent)


def solution(mesh):
    in_specs = (P("row", "col", None), P("row", "col", None), P(), P(None, "row", "col", None))
    out_specs = (P(None, "row", "col", None), P(), P("row", "col", None), P("row", "col", None))
    return jax.shard_map(
        functools.partial(on_device, mesh.shape["row"], mesh.shape["col"]),
        mesh=mesh, in_specs=in_specs, out_specs=out_specs, check_vma=False,
    )
```

time: 497 us -> 69.5 us (0.14)
  waiting for transfers between devices: 245 us -> 0 us
  matrix products: 93 us -> 0 us
  local copies, waits for them, and re-layouts: 74 us -> 9.11 us
  Pallas kernels: 0 us -> 59.5 us
  starting transfers between devices: 43.3 us -> 0 us
  other arithmetic: 20.8 us -> 0 us
  between operations: 15.6 us -> 0.67 us
    psum x1 -> x0, waiting for transfers between devices: 238 us -> none  [on_device(): weight_grad = lax.psum(local_grad, ('row', 'col')) / math.sqrt(total_cells)]
    pallas_call x0 -> x1, Pallas kernels: none -> 59.5 us  [on_device(): pl.pallas_call(functools.partial(kernel, nrow, ncol, chunk, owners, scale...]
    ppermute x12 -> x0, starting transfers between devices: 43.2 us -> none  [the longest x4 21.7 us: with_halo(): lax.ppermute(tail, axis, [(i, (i + 1) % count) for i in range(ends)])]
    transpose x1 -> x0, matrix products: 42.7 us -> none  [on_device(): local_grad = jnp.transpose(kernel_raw, (1, 2, 3, 0, 4))]
    dot_general x48 -> x0, matrix products: 38.9 us -> none  [the longest x24 25.2 us: on_device(): jnp.einsum('hwg,cg->hwc', grad_volume[disp_index].astype(jnp.float32), gr...]
    convert_element_type x52 -> x0, local copies, waits for them, and re-layouts: 22.1 us -> none  [the longest x50 21.1 us: on_device(): grad_volume = conv_valid(padded_cotangent, flipped).astype(jnp.bfloat16)]
    broadcast_in_dim x5 -> x0, local copies, waits for them, and re-layouts: 20 us -> none  [the longest x2 13.9 us: on_device(): full_pad[None]]
    unnamed x88 -> x10, local copies, waits for them, and re-layouts: 20.9 us -> 5.64 us
  transfers between devices with their start and end apart: 13 -> 0, of which waited for: 5 -> 0; matrix products, arithmetic and copies ran while one was open for 33% -> 0% of each run, Pallas kernels for 0% -> 0%
where the time goes in v1:
time: 69.5 us; the launch traced here: 69.3 us
  Pallas kernels  59.5 us (86%)
  local copies, waits for them, and re-layouts  9.11 us (13%)
    pallas_call x1, Pallas kernels, on_device(): pl.pallas_call(functools.partial(kernel, nrow, ncol, chunk, owners, scale...  59.5 us
    unnamed x10, local copies, waits for them, and re-layouts  5.64 us
    pallas_call x2, local copies, waits for them, and re-layouts, on_device(): pl.pallas_call(functools.partial(kernel, nrow, ncol, chunk, owners, scale...  3.48 us

profile of v1, /device:TPU:1, one launch (start us, length us, event | category | flops | bytes accessed | tf_op | source)
XLA Modules:
  0.0 69.3 jit_solution(6281050995718911228)
XLA Ops:
  0.6 1.8 %copy.8.w_ref = bf16[3,3,3,40,32]{4,3,2,1,0:T(8,128)(2,1)} copy(bf16[3,3,3,40,32]{3,4,2,1,0:T(8,128)(2,1)} %param.6) | data formatting | bytes 138240 | tf_op args[2]
  2.4 2.5 %copy.9.c_ref = bf16[24,4,64,32]{3,2,1,0:T(8,128)(2,1)} copy(bf16[24,4,64,32]{2,3,1,0:T(8,128)(2,1)} %param.7) | data formatting | bytes 786432 | tf_op args[3]
  4.9 59.5 %cost_volume.1 = (bf16[24,4,64,32]{3,2,1,0:T(8,128)(2,1)}, f32[3,3,3,40,32]{4,3,2,1,0:T(8,128)}, bf16[4,64,320]{2,1,0:T(8,128)(2,1)}, bf16[4,64,320]{2,1,0:T(8,128)(2,1)}) custom-call(bf16[4,64,320]{2,1,0:T(8,128)(2,1)} %l_ref.1, bf16[4,64,320]{2,1,0:T(8,128)(2,1)} %r_ref.1, bf16[3,3,3,40,32]{4,3,2,1,0:T(8,128)(2,1)} %copy.8.w_ref, ...), custom_call_target="tpu_custom_call" | custom-call | tf_op jit(solution)/shard_map/cost_volume/pallas_call | solution.py:438
  64.4 0.0 copy-start
  64.4 0.0 copy-start.2
  64.4 0.0 copy-start.1
  64.4 2.5 %copy.10 = bf16[24,4,64,32]{2,3,1,0:T(8,128)(2,1)} copy(bf16[24,4,64,32]{3,2,1,0:T(8,128)(2,1)} %get-tuple-element.4) | data formatting | bytes 786432 | tf_op jit(solution)/shard_map/cost_volume/pallas_call | solution.py:438
  66.9 0.0 copy-done
  66.9 1.0 %copy.11 = f32[3,3,3,40,32]{3,4,2,1,0:T(8,128)} copy(f32[3,3,3,40,32]{4,3,2,1,0:T(8,128)S(1)} %copy-done) | data formatting | bytes 276480 | tf_op jit(solution)/shard_map/cost_volume/pallas_call | solution.py:438
  67.9 0.0 copy-done.2
  67.9 0.7 copy.14
  68.6 0.0 copy-done.1
  68.6 0.7 copy.15
Async XLA Ops:
  64.4 2.5 %copy-start = (f32[3,3,3,40,32]{4,3,2,1,0:T(8,128)S(1)}, f32[3,3,3,40,32]{4,3,2,1,0:T(8,128)}, u32[]{:S(2)}) copy-start(f32[3,3,3,40,32]{4,3,2,1,0:T(8,128)} %get-tuple-element.5) | copy-start | bytes 414724
  64.4 3.5 %copy-start.2 = (bf16[4,64,320]{2,1,0:T(8,128)(2,1)S(1)}, bf16[4,64,320]{2,1,0:T(8,128)(2,1)}, u32[]{:S(2)}) copy-start(bf16[4,64,320]{2,1,0:T(8,128)(2,1)} %get-tuple-element.14) | copy-start | bytes 491524
  64.4 4.2 %copy-start.1 = (bf16[4,64,320]{2,1,0:T(8,128)(2,1)S(1)}, bf16[4,64,320]{2,1,0:T(8,128)(2,1)}, u32[]{:S(2)}) copy-start(bf16[4,64,320]{2,1,0:T(8,128)(2,1)} %get-tuple-element.15) | copy-start | bytes 491524

commit v2 on v1

--- a/solution.py
+++ b/solution.py
@@ -38,7 +38,7 @@
     sem1_s, sem1_r, sem2_s, sem2_r, sem3_s, sem3_r,
 ):
     rows, cols, channels = l_ref.shape
-    groups, feats = w_ref.shape[3], w_ref.shape[4]
+    groups, feats = w_ref.shape[4], w_ref.shape[3]
     group_size = channels // groups
     cells = rows * cols
     row, col = lax.axis_index("row"), lax.axis_index("col")
@@ -131,14 +131,12 @@
                 body[2, k, h] = after.astype(BF)
 
     for k in range(WINDOWS):
-        parts = []
-        for j in range(IN_D):
-            d = OUT_D * k - 1 + j
-            if 0 <= d < DISP:
-                parts.append(c_ref[d].reshape(cells, feats))
-            else:
-                parts.append(jnp.zeros((cells, feats), BF))
-        cs[1, k, 1 : rows + 1] = jnp.concatenate(parts, axis=1).reshape(rows, cols, LANES)
+        for h in range(rows):
+            parts = []
+            for j in range(IN_D):
+                d = OUT_D * k - 1 + j
+                parts.append(c_ref[d, h] if 0 <= d < DISP else jnp.zeros((feats, cols), BF))
+            cs[1, k, 1 + h] = jnp.concatenate(parts, axis=0).T
     fill_edges(edge_c, cs)
     cot_copies = halo_copies(cs, edge_c, halo_c, sem_cs, sem_cr)
     for c in cot_copies:
@@ -148,21 +146,21 @@
     for i in range(OUT_D):
         r = iota((channels, LANES), 0) + i * channels
         sel[i] = jnp.where(r // group_size == iota((channels, LANES), 1), 1.0, 0.0).astype(BF)
-    f_idx = iota((feats, OUT_D * LANES), 0)
-    lane = iota((feats, OUT_D * LANES), 1)
-    banded = jnp.zeros((9 * groups, OUT_D * LANES), F32)
+    g_idx = iota((groups, IN_D * LANES), 0)
+    lane = iota((groups, IN_D * LANES), 1)
+    banded = jnp.zeros((9 * feats, IN_D * LANES), F32)
     for a in range(3):
         tap = jnp.where(
-            (lane % feats == f_idx) & (lane // LANES - (lane % LANES) // feats + 2 == a), 1.0, 0.0
+            (lane % LANES == (lane // LANES + a - 2) * groups + g_idx) & (lane % LANES < OUT_D * groups)
+            & (lane // LANES + a >= 2), 1.0, 0.0
         ).astype(BF)
-        wa = w_ref[a].astype(F32).reshape(9 * groups, feats).astype(BF)
+        wa = w_ref[a].astype(F32).reshape(9 * feats, groups).astype(BF)
         banded = banded + dot(wa, tap)
     for n in range(9):
-        tall = [banded[groups * n : groups * (n + 1), LANES * i : LANES * (i + 1)] for i in range(OUT_D)]
-        tall.append(jnp.zeros((LANES - OUT_D * groups, LANES), F32))
+        tall = [banded[feats * n : feats * (n + 1), LANES * j : LANES * (j + 1)] for j in range(IN_D)]
         tall = jnp.concatenate(tall, axis=0)
-        band_n[LANES * n : LANES * (n + 1)] = tall.astype(BF)
-        band_t[LANES * n : LANES * (n + 1)] = tall.T.astype(BF)
+        band_t[LANES * n : LANES * (n + 1)] = tall.astype(BF)
+        band_n[LANES * n : LANES * (n + 1)] = tall.T.astype(BF)
 
     for c in right_copies:
         c.wait_recv()
@@ -332,15 +330,17 @@
         return carry
 
     lax.fori_loop(0, WINDOWS, forward, 0)
-    for k in range(WINDOWS):
-        for i in range(OUT_D):
-            j = i + 1
-            value = obuf[k, :, feats * j : feats * (j + 1)]
-            if i == 0 and k > 0:
-                value = value + obuf[k - 1, :, feats * (IN_D - 1) : feats * IN_D]
-            if i == OUT_D - 1 and k < WINDOWS - 1:
-                value = value + obuf[k + 1, :, 0:feats]
-            cost_ref[OUT_D * k + i] = value.astype(BF).reshape(rows, cols, feats)
+    for h in range(rows):
+        part = [obuf[k, cols * h : cols * (h + 1)].T for k in range(WINDOWS)]
+        for k in range(WINDOWS):
+            for i in range(OUT_D):
+                j = i + 1
+                value = part[k][feats * j : feats * (j + 1)]
+                if i == 0 and k > 0:
+                    value = value + part[k - 1][feats * (IN_D - 1) : feats * IN_D]
+                if i == OUT_D - 1 and k < WINDOWS - 1:
+                    value = value + part[k + 1][0:feats]
+                cost_ref[OUT_D * k + i, h] = value.astype(BF)
 
     for c in back_copies:
         c.wait_recv()
@@ -364,9 +364,9 @@
     lax.fori_loop(1, ncol, wait3, 0)
     for b in range(3):
         for e in range(3):
-            block = full[groups * (3 * b + e) : groups * (3 * b + e + 1)]
+            block = full[groups * (3 * b + e) : groups * (3 * b + e + 1)].T
             for a in range(3):
-                wg_ref[a, b, e] = block[:, feats * (2 - a) : feats * (3 - a)]
+                wg_ref[a, b, e] = block[feats * (2 - a) : feats * (3 - a)]
 
     for c in right_copies + cot_copies + vol_copies + back_copies:
         c.wait_send()
@@ -398,7 +398,7 @@
 
 def on_device(nrow, ncol, left, right, weight, cotangent):
     rows, cols, channels = left.shape
-    groups, feats = weight.shape[3], weight.shape[4]
+    groups, feats = weight.shape[3:]
     cells = rows * cols
     chunk = -(-9 * groups // ncol)
     chunk = -(-chunk // 16) * 16
@@ -435,11 +435,11 @@
         dma((ncol,)), dma((ncol,)), dma((nrow,)), dma((nrow,)), dma((ncol,)), dma((ncol,)),
     ]
     vmem = pl.BlockSpec(memory_space=pltpu.VMEM)
-    return pl.pallas_call(
+    cost, weight_grad, left_grad, right_grad = pl.pallas_call(
         functools.partial(kernel, nrow, ncol, chunk, owners, scale),
         out_shape=(
-            jax.ShapeDtypeStruct((DISP, rows, cols, feats), BF),
-            jax.ShapeDtypeStruct(weight.shape, F32),
+            jax.ShapeDtypeStruct((DISP, rows, feats, cols), BF),
+            jax.ShapeDtypeStruct((3, 3, 3, feats, groups), F32),
             jax.ShapeDtypeStruct(left.shape, BF),
             jax.ShapeDtypeStruct(right.shape, BF),
         ),
@@ -450,7 +450,8 @@
             collective_id=0, has_side_effects=True, vmem_limit_bytes=56 * 1024 * 1024
         ),
         name="cost_volume",
-    )(left, right, weight, cotangent)
+    )(left, right, jnp.swapaxes(weight, 3, 4), jnp.swapaxes(cotangent, 2, 3))
+    return jnp.swapaxes(cost, 2, 3), jnp.swapaxes(weight_grad, 3, 4), left_grad, right_grad
 
 
 def solution(mesh):

time: 69.5 us -> 64.9 us (0.934)
  local copies, waits for them, and re-layouts: 9.11 us -> 4.9 us
    pallas_call x2 -> x0, local copies, waits for them, and re-layouts: 3.48 us -> none  [on_device(): pl.pallas_call(functools.partial(kernel, nrow, ncol, chunk, owners, scale...]
    unnamed x10, local copies, waits for them, and re-layouts: 5.64 us -> 4.9 us
where the time goes in v2:
time: 64.9 us; the launch traced here: 64.8 us
  Pallas kernels  59.2 us (91%)
  local copies, waits for them, and re-layouts  4.9 us (8%)
  between operations  0.65 us (1%)
    pallas_call x1, Pallas kernels, on_device(): pl.pallas_call(functools.partial(kernel, nrow, ncol, chunk, owners, scale...  59.2 us
    unnamed x10, local copies, waits for them, and re-layouts  4.9 us

profile of v2, /device:TPU:1, one launch (start us, length us, event | category | flops | bytes accessed | tf_op | source)
XLA Modules:
  0.0 64.8 jit_solution(8357495989331676961)
XLA Ops:
  0.6 59.2 %cost_volume.1 = (bf16[24,4,32,64]{3,2,1,0:T(8,128)(2,1)}, f32[3,3,3,32,40]{4,3,2,1,0:T(8,128)}, bf16[4,64,320]{2,1,0:T(8,128)(2,1)}, bf16[4,64,320]{2,1,0:T(8,128)(2,1)}) custom-call(bf16[4,64,320]{2,1,0:T(8,128)(2,1)} %l_ref.1, bf16[4,64,320]{2,1,0:T(8,128)(2,1)} %r_ref.1, bf16[3,3,3,32,40]{4,3,2,1,0:T(8,128)(2,1)} %bitcast.7, bf16[24,4,32,64]{3,2,1,0:T(8,128)(2,1)} %bitcast.5), custom_call_target="tpu_custom_call" | custom-call | tf_op jit(solution)/shard_map/cost_volume/pallas_call | solution.py:438
  59.8 0.0 copy-start
  59.9 2.1 %copy.12 = bf16[24,4,64,32]{2,3,1,0:T(8,128)(2,1)} copy(bf16[24,4,64,32]{2,3,1,0:T(8,128)(2,1)} %bitcast.4) | data formatting | bytes 786432
  62.0 0.0 copy-done
  62.0 0.0 copy-start.2
  62.0 0.8 %copy.13 = f32[3,3,3,40,32]{3,4,2,1,0:T(8,128)} copy(f32[3,3,3,40,32]{3,4,2,1,0:T(8,128)S(1)} %bitcast.6) | data formatting | bytes 276480
  62.8 0.3 copy-done.2
  63.1 0.0 copy-start.1
  63.1 0.7 %copy.14 = bf16[4,64,320]{2,1,0:T(8,128)(2,1)} copy(bf16[4,64,320]{2,1,0:T(8,128)(2,1)S(1)} %copy-done.2) | data formatting | bytes 327680
  63.8 0.3 copy-done.1
  64.1 0.7 %copy.15 = bf16[4,64,320]{2,1,0:T(8,128)(2,1)} copy(bf16[4,64,320]{2,1,0:T(8,128)(2,1)S(1)} %copy-done.1) | data formatting | bytes 327680
Async XLA Ops:
  59.8 2.2 %copy-start = (f32[3,3,3,32,40]{4,3,2,1,0:T(8,128)S(1)}, f32[3,3,3,32,40]{4,3,2,1,0:T(8,128)}, u32[]{:S(2)}) copy-start(f32[3,3,3,32,40]{4,3,2,1,0:T(8,128)} %get-tuple-element.9) | copy-start | bytes 414724
  62.0 1.1 %copy-start.2 = (bf16[4,64,320]{2,1,0:T(8,128)(2,1)S(1)}, bf16[4,64,320]{2,1,0:T(8,128)(2,1)}, u32[]{:S(2)}) copy-start(bf16[4,64,320]{2,1,0:T(8,128)(2,1)} %get-tuple-element.18) | copy-start | bytes 491524
  63.1 1.0 %copy-start.1 = (bf16[4,64,320]{2,1,0:T(8,128)(2,1)S(1)}, bf16[4,64,320]{2,1,0:T(8,128)(2,1)}, u32[]{:S(2)}) copy-start(bf16[4,64,320]{2,1,0:T(8,128)(2,1)} %get-tuple-element.19) | copy-start | bytes 491524

commit v3 on v2

--- a/solution.py
+++ b/solution.py
@@ -29,12 +29,14 @@
 
 
 def kernel(
-    nrow, ncol, chunk, owners, scale,
-    l_ref, r_ref, w_ref, c_ref,
-    cost_ref, wg_ref, lg_ref, rg_ref,
+    nrow, ncol, scale,
+    l_any, r_any, w_any, c_any,
+    cost_any, wg_any, lg_any, rg_any,
+    l_ref, r_ref, w_ref, c_ref, cost_ref, wg_ref, lg_ref, rg_ref,
     rband, rf0, rf4, lf, sel, band_n, band_t, cs, vs, vt, edge_c, edge_v, halo_c, halo_v,
-    gv, spread, racc0, racc4, back_send, back_recv, dsum, slots1, part2, slots2, full, obuf,
-    sem_rs, sem_rr, sem_cs, sem_cr, sem_vs, sem_vr, sem_bs, sem_br,
+    gv, spread, racc0, racc4, back_send, back_recv, dsum, slot_c, half, slots_r, part_m, slots_m,
+    gathered, full, obuf,
+    sem_in, sem_out, sem_rs, sem_rr, sem_cs, sem_cr, sem_vs, sem_vr, sem_bs, sem_br, sem_pair,
     sem1_s, sem1_r, sem2_s, sem2_r, sem3_s, sem3_r,
 ):
     rows, cols, channels = l_ref.shape
@@ -42,26 +44,30 @@
     group_size = channels // groups
     cells = rows * cols
     row, col = lax.axis_index("row"), lax.axis_index("col")
+    pairs = ncol // 2
+    pair, core = col // 2, lax.rem(col, 2)
+    mate = (row, col + 1 - 2 * core)
+    halfrows = dsum.shape[0] // 2
+    chunk = halfrows // nrow
 
     def at(dr, dc):
         return (lax.rem(row + dr + nrow, nrow), lax.rem(col + dc + ncol, ncol))
 
+    def along(step):
+        return (row, lax.rem(pair + step, pairs) * 2 + core)
+
     barrier = pltpu.get_barrier_semaphore()
-
-    def hello_col(step, carry):
-        pl.semaphore_signal(barrier, inc=1, device_id=at(0, step), device_id_type=MESH)
-        return carry
-
-    def hello_row(step, carry):
-        pl.semaphore_signal(barrier, inc=1, device_id=at(step, 0), device_id_type=MESH)
-        return carry
-
-    lax.fori_loop(1, ncol, hello_col, 0)
-    lax.fori_loop(1, nrow, hello_row, 0)
-    for dr, dc in NEIGHBOURS:
-        if dr != 0 and dc != 0:
-            pl.semaphore_signal(barrier, inc=1, device_id=at(dr, dc), device_id_type=MESH)
-    pl.semaphore_wait(barrier, ncol - 1 + nrow - 1 + 4)
+    partners = [at(dr, dc) for dr, dc in NEIGHBOURS if dc != 0]
+    partners += [at(step, 0) for step in range(1, nrow)] + [along(step) for step in range(1, pairs)]
+    for partner in partners:
+        pl.semaphore_signal(barrier, inc=1, device_id=partner, device_id_type=MESH)
+    loads = [
+        pltpu.make_async_copy(src, dst, sem_in.at[n])
+        for n, (src, dst) in enumerate(((c_any, c_ref), (w_any, w_ref), (l_any, l_ref), (r_any, r_ref)))
+    ]
+    for load in loads:
+        load.start()
+    pl.semaphore_wait(barrier, len(partners))
 
     def copy(src, dst, send, recv, target):
         return pltpu.make_async_remote_copy(
@@ -69,12 +75,17 @@
             device_id=target, device_id_type=MESH,
         )
 
-    right_copies = [
-        copy(r_ref, rband.at[:, 32:96], sem_rs.at[0], sem_rr.at[0], at(0, 1)),
-        copy(r_ref.at[:, cols - 32 : cols], rband.at[:, 0:32], sem_rs.at[1], sem_rr.at[1], at(0, 2)),
-    ]
-    for c in right_copies:
-        c.start()
+    tail = r_any.at[:, cols - 32 : cols]
+    near = copy(tail, rband.at[:, 64:96], sem_rs.at[0], sem_rr.at[0], at(0, 1))
+    middle = copy(r_any.at[:, 0:32], rband.at[:, 32:64], sem_rs.at[1], sem_rr.at[1], at(0, 1))
+    beyond = copy(tail, rband.at[:, 0:32], sem_rs.at[2], sem_rr.at[2], at(0, 2))
+    forward_near = copy(rband.at[:, 64:96], rband.at[:, 0:32], sem_rs.at[3], sem_rr.at[2], mate)
+    near.start()
+    middle.start()
+
+    @pl.when(core == 0)
+    def _():
+        beyond.start()
 
     def halo_copies(body, edge, halo, send, recv):
         out = []
@@ -130,6 +141,7 @@
                 body[0, k, h] = before.astype(BF)
                 body[2, k, h] = after.astype(BF)
 
+    loads[0].wait()
     for k in range(WINDOWS):
         for h in range(rows):
             parts = []
@@ -142,6 +154,9 @@
     for c in cot_copies:
         c.start()
 
+    loads[1].wait()
+    loads[2].wait()
+    loads[3].wait()
     lf[...] = l_ref[...].astype(F32)
     for i in range(OUT_D):
         r = iota((channels, LANES), 0) + i * channels
@@ -162,21 +177,27 @@
         band_t[LANES * n : LANES * (n + 1)] = tall.astype(BF)
         band_n[LANES * n : LANES * (n + 1)] = tall.T.astype(BF)
 
-    for c in right_copies:
+    for c in cot_copies:
         c.wait_recv()
-    @pl.when(col < 1)
-    def _():
-        rband[:, 32:96] = jnp.zeros((rows, 64, channels), BF)
-
-    @pl.when(col < 2)
-    def _():
-        rband[:, 0:32] = jnp.zeros((rows, 32, channels), BF)
-
-    for h in range(rows):
-        rf0[h, 0:96] = rband[h].astype(F32)
-        rf0[h, 96:160] = r_ref[h].astype(F32)
-        rf4[h, 0:152] = rf0[h, 4:156]
-        rf4[h, 152:160] = rf0[h, 152:160]
+    clear_outside(cs, halo_c)
+    write_shifts(cs, halo_c)
+
+    def grad_volume(k, carry):
+        taps = []
+        for b in range(3):
+            for e in range(3):
+                taps.append(cs[2 - e, k, 2 - b : 2 - b + rows].reshape(cells, LANES))
+        gv[k] = dot(jnp.concatenate(taps, axis=1), band_t[...]).astype(BF)
+        return carry
+
+    lax.fori_loop(0, WINDOWS, grad_volume, 0)
+
+    def widen(start, inside):
+        for h in range(rows):
+            block = rband[h, start : start + 32].astype(F32)
+            rf0[h, start : start + 32] = jnp.where(inside, block, 0.0)
+            stop = 152 if start == 64 else start + 32
+            rf4[h, start:stop] = rf0[h, start + 4 : stop + 4]
 
     def shifted(k, i, h=None):
         start = pl.multiple_of(96 - STEP * (OUT_D * k + i) - (STEP if i % 2 else 0), 8)
@@ -195,16 +216,26 @@
         vt[k] = acc.T
         return carry
 
-    lax.fori_loop(0, WINDOWS, volume, 0)
+    for h in range(rows):
+        rf0[h, 96:160] = r_ref[h].astype(F32)
+    near.wait_recv()
+
+    @pl.when(core == 0)
+    def _():
+        forward_near.start()
+
+    widen(64, col > 0)
+    lax.fori_loop(0, 1, volume, 0)
+    middle.wait_recv()
+    widen(32, col > 0)
+    lax.fori_loop(1, 2, volume, 0)
+    beyond.wait_recv()
+    widen(0, col > 1)
+    lax.fori_loop(2, WINDOWS, volume, 0)
     fill_edges(edge_v, vs)
     vol_copies = halo_copies(vs, edge_v, halo_v, sem_vs, sem_vr)
     for c in vol_copies:
         c.start()
-
-    for c in cot_copies:
-        c.wait_recv()
-    clear_outside(cs, halo_c)
-    write_shifts(cs, halo_c)
 
     dsum[9 * groups :] = jnp.zeros((dsum.shape[0] - 9 * groups, 128), F32)
 
@@ -221,52 +252,12 @@
 
     lax.fori_loop(0, 9, kernel_grad, 0)
 
-    own_rows = pl.ds(pl.multiple_of(col * chunk, 8), chunk)
-
-    def send1(step, carry):
-        r, c = at(0, step)
-
-        @pl.when(c < owners)
-        def _():
-            copy(
-                dsum.at[pl.ds(pl.multiple_of(c * chunk, 8), chunk)], slots1.at[col],
-                sem1_s.at[step], sem1_r.at[col], (r, c),
-            ).start()
-        return carry
-
-    lax.fori_loop(1, ncol, send1, 0)
-
-    def grad_volume(k, carry):
-        taps = []
-        for b in range(3):
-            for e in range(3):
-                taps.append(cs[2 - e, k, 2 - b : 2 - b + rows].reshape(cells, LANES))
-        gv[k] = dot(jnp.concatenate(taps, axis=1), band_t[...]).astype(BF)
-        return carry
-
-    lax.fori_loop(0, WINDOWS, grad_volume, 0)
-
-    @pl.when(col < owners)
-    def _():
-        slots1[col] = dsum[own_rows]
-
-        def wait1(step, carry):
-            _, c = at(0, step)
-            copy(slots1.at[c], slots1.at[c], sem1_s.at[step], sem1_r.at[c], at(0, step)).wait_recv()
-            return carry
-
-        lax.fori_loop(1, ncol, wait1, 0)
-        total = slots1[0]
-        for q in range(1, ncol):
-            total = total + slots1[q]
-        part2[...] = total
-        slots2[row] = total
-
-        def send2(step, carry):
-            copy(part2, slots2.at[row], sem2_s.at[step], sem2_r.at[row], at(step, 0)).start()
-            return carry
-
-        lax.fori_loop(1, nrow, send2, 0)
+    my_half = pl.ds(pl.multiple_of(core * halfrows, 16), halfrows)
+    pair_copy = copy(
+        dsum.at[pl.ds(pl.multiple_of((1 - core) * halfrows, 16), halfrows)], slot_c,
+        sem_pair.at[0], sem_pair.at[1], mate,
+    )
+    pair_copy.start()
 
     racc0[...] = jnp.zeros_like(racc0)
     racc4[...] = jnp.zeros_like(racc4)
@@ -284,9 +275,24 @@
                 acc[h, pl.ds(start, cols)] += s * lf[h]
         return carry
 
-    lax.fori_loop(0, WINDOWS, feature_grads, 0)
+    lax.fori_loop(0, 2, feature_grads, 0)
+
+    pair_copy.wait_recv()
+    half[...] = dsum[my_half] + slot_c[...]
+    row_copies = []
+    for step in range(1, nrow):
+        target = at(step, 0)
+        row_copies.append(copy(
+            half.at[pl.ds(pl.multiple_of(target[0] * chunk, 8), chunk)], slots_r.at[row],
+            sem1_s.at[step], sem1_r.at[row], target,
+        ))
+        row_copies[-1].start()
+    slots_r[row] = half[pl.ds(pl.multiple_of(row * chunk, 8), chunk)]
+    lax.fori_loop(2, WINDOWS, feature_grads, 0)
     inv = 1.0 / group_size
     lg_ref[...] = (lacc[...] * inv).reshape(rows, cols, channels).astype(BF)
+    left_out = pltpu.make_async_copy(lg_ref, lg_any, sem_out.at[2])
+    left_out.start()
     for h in range(rows):
         racc0[h, 4:156] += racc4[h, 0:152]
         back_send[h] = racc0[h, 0:96].astype(BF)
@@ -297,24 +303,20 @@
     for c in back_copies:
         c.start()
 
-    @pl.when(col < owners)
-    def _():
-        def wait2(step, carry):
-            r, _ = at(step, 0)
-            copy(part2, slots2.at[r], sem2_s.at[step], sem2_r.at[r], at(step, 0)).wait_recv()
-            return carry
-
-        lax.fori_loop(1, nrow, wait2, 0)
-        total = slots2[0]
-        for q in range(1, nrow):
-            total = total + slots2[q]
-        full[own_rows] = total * scale
-
-        def send3(step, carry):
-            copy(full.at[own_rows], full.at[own_rows], sem3_s.at[step], sem3_r.at[col], at(0, step)).start()
-            return carry
-
-        lax.fori_loop(1, ncol, send3, 0)
+    for step in range(1, nrow):
+        r = at(step, 0)[0]
+        copy(slots_r.at[r], slots_r.at[r], sem1_s.at[step], sem1_r.at[r], at(step, 0)).wait_recv()
+    total = slots_r[0]
+    for q in range(1, nrow):
+        total = total + slots_r[q]
+    if part_m.shape[0] > chunk:
+        total = jnp.concatenate([total, jnp.zeros((part_m.shape[0] - chunk, 128), F32)], axis=0)
+    part_m[...] = total.astype(BF)
+    col_copies = []
+    for step in range(1, pairs):
+        col_copies.append(copy(part_m, slots_m.at[pair], sem2_s.at[step], sem2_r.at[pair], along(step)))
+        col_copies[-1].start()
+    slots_m[pair] = part_m[...]
 
     for c in vol_copies:
         c.wait_recv()
@@ -330,6 +332,20 @@
         return carry
 
     lax.fori_loop(0, WINDOWS, forward, 0)
+
+    for step in range(1, pairs):
+        p = lax.rem(pair + step, pairs)
+        copy(part_m, slots_m.at[p], sem2_s.at[step], sem2_r.at[p], along(step)).wait_recv()
+    total = slots_m[0].astype(F32)
+    for q in range(1, pairs):
+        total = total + slots_m[q].astype(F32)
+    gathered[core, row] = (total * scale).astype(BF)
+    gather_copies = []
+    for step in range(1, nrow):
+        mine = gathered.at[core, row]
+        gather_copies.append(copy(mine, mine, sem3_s.at[step], sem3_r.at[row], at(step, 0)))
+        gather_copies[-1].start()
+
     for h in range(rows):
         part = [obuf[k, cols * h : cols * (h + 1)].T for k in range(WINDOWS)]
         for k in range(WINDOWS):
@@ -341,74 +357,71 @@
                 if i == OUT_D - 1 and k < WINDOWS - 1:
                     value = value + part[k + 1][0:feats]
                 cost_ref[OUT_D * k + i, h] = value.astype(BF)
+    cost_out = pltpu.make_async_copy(cost_ref, cost_any, sem_out.at[0])
+    cost_out.start()
 
     for c in back_copies:
         c.wait_recv()
-    near = jnp.where(col < ncol - 1, 1.0, 0.0).astype(F32)
-    far = jnp.where(col < ncol - 2, 1.0, 0.0).astype(F32)
     for h in range(rows):
-        own = racc0[h, 96:160] + near * back_recv[h, 0:64].astype(F32)
-        tail = own[32:64] + far * back_recv[h, 64:96].astype(F32)
+        own = racc0[h, 96:160] + jnp.where(col < ncol - 1, back_recv[h, 0:64].astype(F32), 0.0)
+        last = own[32:64] + jnp.where(col < ncol - 2, back_recv[h, 64:96].astype(F32), 0.0)
         rg_ref[h, 0:32] = (own[0:32] * inv).astype(BF)
-        rg_ref[h, 32:64] = (tail * inv).astype(BF)
-
-    def wait3(step, carry):
-        _, c = at(0, step)
-
-        @pl.when(c < owners)
-        def _():
-            piece = full.at[pl.ds(pl.multiple_of(c * chunk, 8), chunk)]
-            copy(piece, piece, sem3_s.at[step], sem3_r.at[c], at(0, step)).wait_recv()
-        return carry
-
-    lax.fori_loop(1, ncol, wait3, 0)
+        rg_ref[h, 32:64] = (last * inv).astype(BF)
+    right_out = pltpu.make_async_copy(rg_ref, rg_any, sem_out.at[1])
+    right_out.start()
+
+    for step in range(1, nrow):
+        r = at(step, 0)[0]
+        theirs = gathered.at[core, r]
+        copy(theirs, theirs, sem3_s.at[step], sem3_r.at[r], at(step, 0)).wait_recv()
+    mate_copy = copy(gathered.at[core], gathered.at[core], sem_pair.at[2], sem_pair.at[3], mate)
+    mate_copy.start()
+    mate_copy.wait_recv()
+    for side in range(2):
+        for r in range(nrow):
+            start = side * halfrows + r * chunk
+            full[start : start + chunk] = gathered[side, r].astype(F32)[0:chunk]
     for b in range(3):
         for e in range(3):
             block = full[groups * (3 * b + e) : groups * (3 * b + e + 1)].T
             for a in range(3):
                 wg_ref[a, b, e] = block[feats * (2 - a) : feats * (3 - a)]
 
-    for c in right_copies + cot_copies + vol_copies + back_copies:
+    weight_out = pltpu.make_async_copy(wg_ref, wg_any, sem_out.at[3])
+    weight_out.start()
+
+    @pl.when(core == 0)
+    def _():
+        beyond.wait_send()
+        forward_near.wait_send()
+
+    sent = [near, middle, pair_copy, mate_copy] + cot_copies + vol_copies + back_copies
+    for c in sent + row_copies + col_copies + gather_copies:
         c.wait_send()
-
-    def sent1(step, carry):
-        _, c = at(0, step)
-
-        @pl.when(c < owners)
-        def _():
-            copy(dsum.at[own_rows], slots1.at[col], sem1_s.at[step], sem1_r.at[col], at(0, step)).wait_send()
-        return carry
-
-    lax.fori_loop(1, ncol, sent1, 0)
-
-    @pl.when(col < owners)
-    def _():
-        def sent2(step, carry):
-            copy(part2, slots2.at[row], sem2_s.at[step], sem2_r.at[row], at(step, 0)).wait_send()
-            return carry
-
-        lax.fori_loop(1, nrow, sent2, 0)
-
-        def sent3(step, carry):
-            copy(full.at[own_rows], full.at[own_rows], sem3_s.at[step], sem3_r.at[col], at(0, step)).wait_send()
-            return carry
-
-        lax.fori_loop(1, ncol, sent3, 0)
+    for c in (cost_out, right_out, left_out, weight_out):
+        c.wait()
 
 
 def on_device(nrow, ncol, left, right, weight, cotangent):
     rows, cols, channels = left.shape
     groups, feats = weight.shape[3:]
     cells = rows * cols
-    chunk = -(-9 * groups // ncol)
-    chunk = -(-chunk // 16) * 16
-    owners = -(-9 * groups // chunk)
+    halfrows = -(-9 * groups // (16 * nrow)) * 8 * nrow
+    chunk = halfrows // nrow
+    slab = -(-chunk // 16) * 16
     scale = 1.0 / math.sqrt(DISP * rows * nrow * cols * ncol)
     dma = pltpu.SemaphoreType.DMA
     body = pltpu.VMEM((3, WINDOWS, rows + 2, cols, LANES), BF)
     edge = pltpu.VMEM((2, 16, LANES), BF)
     halo = pltpu.VMEM((2, 3, 16, LANES), BF)
-    scratch = [
+    outs = (
+        jax.ShapeDtypeStruct((DISP, rows, feats, cols), BF),
+        jax.ShapeDtypeStruct((3, 3, 3, feats, groups), F32),
+        jax.ShapeDtypeStruct(left.shape, BF),
+        jax.ShapeDtypeStruct(right.shape, BF),
+    )
+    args = (left, right, jnp.swapaxes(weight, 3, 4), jnp.swapaxes(cotangent, 2, 3))
+    scratch = [pltpu.VMEM(a.shape, a.dtype) for a in args + outs] + [
         pltpu.VMEM((rows, 96, channels), BF),
         pltpu.VMEM((rows, 160, channels), F32),
         pltpu.VMEM((rows, 160, channels), F32),
@@ -425,32 +438,31 @@
         pltpu.VMEM((rows, 160, channels), F32),
         pltpu.VMEM((rows, 96, channels), BF),
         pltpu.VMEM((rows, 96, channels), BF),
-        pltpu.VMEM((ncol * chunk, 128), F32),
-        pltpu.VMEM((ncol, chunk, 128), F32),
-        pltpu.VMEM((chunk, 128), F32),
+        pltpu.VMEM((2 * halfrows, 128), F32),
+        pltpu.VMEM((halfrows, 128), F32),
+        pltpu.VMEM((halfrows, 128), F32),
         pltpu.VMEM((nrow, chunk, 128), F32),
-        pltpu.VMEM((ncol * chunk, 128), F32),
+        pltpu.VMEM((slab, 128), BF),
+        pltpu.VMEM((ncol // 2, slab, 128), BF),
+        pltpu.VMEM((2, nrow, slab, 128), BF),
+        pltpu.VMEM((2 * halfrows, 128), F32),
         pltpu.VMEM((WINDOWS, cells, LANES), F32),
-        dma((2,)), dma((2,)), dma((8,)), dma((8,)), dma((8,)), dma((8,)), dma((2,)), dma((2,)),
-        dma((ncol,)), dma((ncol,)), dma((nrow,)), dma((nrow,)), dma((ncol,)), dma((ncol,)),
+        dma((4,)), dma((4,)), dma((4,)), dma((3,)), dma((8,)), dma((8,)), dma((8,)), dma((8,)),
+        dma((2,)), dma((2,)), dma((4,)),
+        dma((nrow,)), dma((nrow,)), dma((ncol // 2,)), dma((ncol // 2,)), dma((nrow,)), dma((nrow,)),
     ]
-    vmem = pl.BlockSpec(memory_space=pltpu.VMEM)
+    anywhere = pl.BlockSpec(memory_space=pl.ANY)
     cost, weight_grad, left_grad, right_grad = pl.pallas_call(
-        functools.partial(kernel, nrow, ncol, chunk, owners, scale),
-        out_shape=(
-            jax.ShapeDtypeStruct((DISP, rows, feats, cols), BF),
-            jax.ShapeDtypeStruct((3, 3, 3, feats, groups), F32),
-            jax.ShapeDtypeStruct(left.shape, BF),
-            jax.ShapeDtypeStruct(right.shape, BF),
-        ),
-        in_specs=[vmem] * 4,
-        out_specs=(vmem,) * 4,
+        functools.partial(kernel, nrow, ncol, scale),
+        out_shape=outs,
+        in_specs=[anywhere] * 4,
+        out_specs=(anywhere,) * 4,
         scratch_shapes=scratch,
         compiler_params=pltpu.CompilerParams(
             collective_id=0, has_side_effects=True, vmem_limit_bytes=56 * 1024 * 1024
         ),
         name="cost_volume",
-    )(left, right, jnp.swapaxes(weight, 3, 4), jnp.swapaxes(cotangent, 2, 3))
+    )(*args)
     return jnp.swapaxes(cost, 2, 3), jnp.swapaxes(weight_grad, 3, 4), left_grad, right_grad
 
 

time: 64.9 us -> 57.2 us (0.88)
  Pallas kernels: 59.2 us -> 51.5 us
    pallas_call x1, Pallas kernels: 59.2 us -> 51.5 us  [on_device(): pl.pallas_call(functools.partial(kernel, nrow, ncol, scale), out_shape=ou...]
where the time goes in v3:
time: 57.2 us; the launch traced here: 57.1 us
  Pallas kernels  51.5 us (90%)
  local copies, waits for them, and re-layouts  4.9 us (9%)
  between operations  0.65 us (1%)
    pallas_call x1, Pallas kernels, on_device(): pl.pallas_call(functools.partial(kernel, nrow, ncol, scale), out_shape=ou...  51.5 us
    unnamed x10, local copies, waits for them, and re-layouts  4.9 us

profile of v3, /device:TPU:1, one launch (start us, length us, event | category | flops | bytes accessed | tf_op | source)
XLA Modules:
  0.0 57.1 jit_solution(10364691024315319147)
XLA Ops:
  0.6 51.5 %cost_volume.1 = (bf16[24,4,32,64]{3,2,1,0:T(8,128)(2,1)}, f32[3,3,3,32,40]{4,3,2,1,0:T(8,128)}, bf16[4,64,320]{2,1,0:T(8,128)(2,1)}, bf16[4,64,320]{2,1,0:T(8,128)(2,1)}) custom-call(bf16[4,64,320]{2,1,0:T(8,128)(2,1)} %l_any.1, bf16[4,64,320]{2,1,0:T(8,128)(2,1)} %r_any.1, bf16[3,3,3,32,40]{4,3,2,1,0:T(8,128)(2,1)} %bitcast.7, bf16[24,4,32,64]{3,2,1,0:T(8,128)(2,1)} %bitcast.5), custom_call_target="tpu_custom_call" | custom-call | tf_op jit(solution)/shard_map/cost_volume/pallas_call | solution.py:455
  52.2 0.0 copy-start
  52.2 2.1 %copy.12 = bf16[24,4,64,32]{2,3,1,0:T(8,128)(2,1)} copy(bf16[24,4,64,32]{2,3,1,0:T(8,128)(2,1)} %bitcast.4) | data formatting | bytes 786432
  54.3 0.0 copy-done
  54.3 0.0 copy-start.2
  54.3 0.8 %copy.13 = f32[3,3,3,40,32]{3,4,2,1,0:T(8,128)} copy(f32[3,3,3,40,32]{3,4,2,1,0:T(8,128)S(1)} %bitcast.6) | data formatting | bytes 276480
  55.1 0.3 copy-done.2
  55.4 0.0 copy-start.1
  55.4 0.7 %copy.14 = bf16[4,64,320]{2,1,0:T(8,128)(2,1)} copy(bf16[4,64,320]{2,1,0:T(8,128)(2,1)S(1)} %copy-done.2) | data formatting | bytes 327680
  56.1 0.3 copy-done.1
  56.4 0.7 %copy.15 = bf16[4,64,320]{2,1,0:T(8,128)(2,1)} copy(bf16[4,64,320]{2,1,0:T(8,128)(2,1)S(1)} %copy-done.1) | data formatting | bytes 327680
Async XLA Ops:
  52.2 2.2 %copy-start = (f32[3,3,3,32,40]{4,3,2,1,0:T(8,128)S(1)}, f32[3,3,3,32,40]{4,3,2,1,0:T(8,128)}, u32[]{:S(2)}) copy-start(f32[3,3,3,32,40]{4,3,2,1,0:T(8,128)} %get-tuple-element.9) | copy-start | bytes 414724
  54.3 1.1 %copy-start.2 = (bf16[4,64,320]{2,1,0:T(8,128)(2,1)S(1)}, bf16[4,64,320]{2,1,0:T(8,128)(2,1)}, u32[]{:S(2)}) copy-start(bf16[4,64,320]{2,1,0:T(8,128)(2,1)} %get-tuple-element.18) | copy-start | bytes 491524
  55.4 1.0 %copy-start.1 = (bf16[4,64,320]{2,1,0:T(8,128)(2,1)S(1)}, bf16[4,64,320]{2,1,0:T(8,128)(2,1)}, u32[]{:S(2)}) copy-start(bf16[4,64,320]{2,1,0:T(8,128)(2,1)} %get-tuple-element.19) | copy-start | bytes 491524

commit v4 on v3

--- a/solution.py
+++ b/solution.py
@@ -31,12 +31,12 @@
 def kernel(
     nrow, ncol, scale,
     l_any, r_any, w_any, c_any,
-    cost_any, wg_any, lg_any, rg_any,
-    l_ref, r_ref, w_ref, c_ref, cost_ref, wg_ref, lg_ref, rg_ref,
+    cost_ref, wg_ref, lg_ref, rg_ref,
+    l_ref, r_ref, w_ref, c_ref,
     rband, rf0, rf4, lf, sel, band_n, band_t, cs, vs, vt, edge_c, edge_v, halo_c, halo_v,
     gv, spread, racc0, racc4, back_send, back_recv, dsum, slot_c, half, slots_r, part_m, slots_m,
     gathered, full, obuf,
-    sem_in, sem_out, sem_rs, sem_rr, sem_cs, sem_cr, sem_vs, sem_vr, sem_bs, sem_br, sem_pair,
+    sem_in, sem_rs, sem_rr, sem_cs, sem_cr, sem_vs, sem_vr, sem_bs, sem_br, sem_pair,
     sem1_s, sem1_r, sem2_s, sem2_r, sem3_s, sem3_r,
 ):
     rows, cols, channels = l_ref.shape
@@ -177,21 +177,6 @@
         band_t[LANES * n : LANES * (n + 1)] = tall.astype(BF)
         band_n[LANES * n : LANES * (n + 1)] = tall.T.astype(BF)
 
-    for c in cot_copies:
-        c.wait_recv()
-    clear_outside(cs, halo_c)
-    write_shifts(cs, halo_c)
-
-    def grad_volume(k, carry):
-        taps = []
-        for b in range(3):
-            for e in range(3):
-                taps.append(cs[2 - e, k, 2 - b : 2 - b + rows].reshape(cells, LANES))
-        gv[k] = dot(jnp.concatenate(taps, axis=1), band_t[...]).astype(BF)
-        return carry
-
-    lax.fori_loop(0, WINDOWS, grad_volume, 0)
-
     def widen(start, inside):
         for h in range(rows):
             block = rband[h, start : start + 32].astype(F32)
@@ -213,7 +198,7 @@
             acc = acc + dot(product, sel[i])
         acc = (acc * (1.0 / group_size)).astype(BF)
         vs[1, k, 1 : rows + 1] = acc.reshape(rows, cols, LANES)
-        vt[k] = acc.T
+        vt[:, pl.ds(pl.multiple_of(k * cells, 128), cells)] = acc.T
         return carry
 
     for h in range(rows):
@@ -237,20 +222,26 @@
     for c in vol_copies:
         c.start()
 
+    for c in cot_copies:
+        c.wait_recv()
+    clear_outside(cs, halo_c)
+    write_shifts(cs, halo_c)
+
     dsum[9 * groups :] = jnp.zeros((dsum.shape[0] - 9 * groups, 128), F32)
 
-    def kernel_grad(n, carry):
-        t, hb = 2 - n % 3, 2 - n // 3
-        acc = jnp.zeros((LANES, LANES), F32)
-        for k in range(WINDOWS):
-            acc = acc + dot(vt[k], cs[t, k, pl.ds(hb, rows)].reshape(cells, LANES))
-        total = acc[0:groups]
-        for i in range(1, OUT_D):
-            total = total + pltpu.roll(acc[groups * i : groups * (i + 1)], LANES - feats * i, 1)
-        dsum[pl.ds(pl.multiple_of(n * groups, 8), groups)] = total[:, 0:128]
+    def kernel_grad(b, carry):
+        for e in range(3):
+            right = jnp.concatenate(
+                [cs[2 - e, k, pl.ds(2 - b, rows)].reshape(cells, LANES) for k in range(WINDOWS)], axis=0
+            )
+            acc = dot(vt[...], right)
+            total = acc[0:groups]
+            for i in range(1, OUT_D):
+                total = total + pltpu.roll(acc[groups * i : groups * (i + 1)], LANES - feats * i, 1)
+            dsum[pl.ds(pl.multiple_of((3 * b + e) * groups, 8), groups)] = total[:, 0:128]
         return carry
 
-    lax.fori_loop(0, 9, kernel_grad, 0)
+    lax.fori_loop(0, 3, kernel_grad, 0)
 
     my_half = pl.ds(pl.multiple_of(core * halfrows, 16), halfrows)
     pair_copy = copy(
@@ -259,23 +250,15 @@
     )
     pair_copy.start()
 
-    racc0[...] = jnp.zeros_like(racc0)
-    racc4[...] = jnp.zeros_like(racc4)
-    lacc = spread.at[0]
-    lacc[...] = jnp.zeros((cells, channels), F32)
-
-    def feature_grads(k, carry):
-        for i in range(OUT_D):
-            spread[1] = dot(gv[k], sel[i], ((1,), (1,)))
-            start = pl.multiple_of(96 - STEP * (OUT_D * k + i) - (STEP if i % 2 else 0), 8)
-            acc = racc4 if i % 2 else racc0
-            for h in range(rows):
-                s = spread[1, cols * h : cols * (h + 1)]
-                lacc[cols * h : cols * (h + 1)] += s * shifted(k, i, h)
-                acc[h, pl.ds(start, cols)] += s * lf[h]
+    def grad_volume(k, carry):
+        taps = []
+        for b in range(3):
+            for e in range(3):
+                taps.append(cs[2 - e, k, 2 - b : 2 - b + rows].reshape(cells, LANES))
+        gv[k] = dot(jnp.concatenate(taps, axis=1), band_t[...]).astype(BF)
         return carry
 
-    lax.fori_loop(0, 2, feature_grads, 0)
+    lax.fori_loop(0, WINDOWS, grad_volume, 0)
 
     pair_copy.wait_recv()
     half[...] = dsum[my_half] + slot_c[...]
@@ -288,20 +271,23 @@
         ))
         row_copies[-1].start()
     slots_r[row] = half[pl.ds(pl.multiple_of(row * chunk, 8), chunk)]
-    lax.fori_loop(2, WINDOWS, feature_grads, 0)
-    inv = 1.0 / group_size
-    lg_ref[...] = (lacc[...] * inv).reshape(rows, cols, channels).astype(BF)
-    left_out = pltpu.make_async_copy(lg_ref, lg_any, sem_out.at[2])
-    left_out.start()
-    for h in range(rows):
-        racc0[h, 4:156] += racc4[h, 0:152]
-        back_send[h] = racc0[h, 0:96].astype(BF)
-    back_copies = [
-        copy(back_send.at[:, 32:96], back_recv.at[:, 0:64], sem_bs.at[0], sem_br.at[0], at(0, -1)),
-        copy(back_send.at[:, 0:32], back_recv.at[:, 64:96], sem_bs.at[1], sem_br.at[1], at(0, -2)),
-    ]
-    for c in back_copies:
-        c.start()
+    racc0[...] = jnp.zeros_like(racc0)
+    racc4[...] = jnp.zeros_like(racc4)
+    lacc = spread.at[0]
+    lacc[...] = jnp.zeros((cells, channels), F32)
+
+    def feature_grads(k, carry):
+        for i in range(OUT_D):
+            spread[1] = dot(gv[k], sel[i], ((1,), (1,)))
+            start = pl.multiple_of(96 - STEP * (OUT_D * k + i) - (STEP if i % 2 else 0), 8)
+            acc = racc4 if i % 2 else racc0
+            for h in range(rows):
+                s = spread[1, cols * h : cols * (h + 1)]
+                lacc[cols * h : cols * (h + 1)] += s * shifted(k, i, h)
+                acc[h, pl.ds(start, cols)] += s * lf[h]
+        return carry
+
+    lax.fori_loop(0, 2, feature_grads, 0)
 
     for step in range(1, nrow):
         r = at(step, 0)[0]
@@ -318,6 +304,19 @@
         col_copies[-1].start()
     slots_m[pair] = part_m[...]
 
+    lax.fori_loop(2, WINDOWS, feature_grads, 0)
+    inv = 1.0 / group_size
+    lg_ref[...] = (lacc[...] * inv).reshape(rows, cols, channels).astype(BF)
+    for h in range(rows):
+        racc0[h, 4:156] += racc4[h, 0:152]
+        back_send[h] = racc0[h, 0:96].astype(BF)
+    back_copies = [
+        copy(back_send.at[:, 32:96], back_recv.at[:, 0:64], sem_bs.at[0], sem_br.at[0], at(0, -1)),
+        copy(back_send.at[:, 0:32], back_recv.at[:, 64:96], sem_bs.at[1], sem_br.at[1], at(0, -2)),
+    ]
+    for c in back_copies:
+        c.start()
+
     for c in vol_copies:
         c.wait_recv()
     clear_outside(vs, halo_v)
@@ -331,7 +330,7 @@
         obuf[k] = dot(jnp.concatenate(taps, axis=1), band_n[...])
         return carry
 
-    lax.fori_loop(0, WINDOWS, forward, 0)
+    lax.fori_loop(0, 2, forward, 0)
 
     for step in range(1, pairs):
         p = lax.rem(pair + step, pairs)
@@ -346,6 +345,8 @@
         gather_copies.append(copy(mine, mine, sem3_s.at[step], sem3_r.at[row], at(step, 0)))
         gather_copies[-1].start()
 
+    lax.fori_loop(2, WINDOWS, forward, 0)
+
     for h in range(rows):
         part = [obuf[k, cols * h : cols * (h + 1)].T for k in range(WINDOWS)]
         for k in range(WINDOWS):
@@ -357,8 +358,6 @@
                 if i == OUT_D - 1 and k < WINDOWS - 1:
                     value = value + part[k + 1][0:feats]
                 cost_ref[OUT_D * k + i, h] = value.astype(BF)
-    cost_out = pltpu.make_async_copy(cost_ref, cost_any, sem_out.at[0])
-    cost_out.start()
 
     for c in back_copies:
         c.wait_recv()
@@ -367,8 +366,6 @@
         last = own[32:64] + jnp.where(col < ncol - 2, back_recv[h, 64:96].astype(F32), 0.0)
         rg_ref[h, 0:32] = (own[0:32] * inv).astype(BF)
         rg_ref[h, 32:64] = (last * inv).astype(BF)
-    right_out = pltpu.make_async_copy(rg_ref, rg_any, sem_out.at[1])
-    right_out.start()
 
     for step in range(1, nrow):
         r = at(step, 0)[0]
@@ -387,8 +384,6 @@
             for a in range(3):
                 wg_ref[a, b, e] = block[feats * (2 - a) : feats * (3 - a)]
 
-    weight_out = pltpu.make_async_copy(wg_ref, wg_any, sem_out.at[3])
-    weight_out.start()
 
     @pl.when(core == 0)
     def _():
@@ -398,8 +393,6 @@
     sent = [near, middle, pair_copy, mate_copy] + cot_copies + vol_copies + back_copies
     for c in sent + row_copies + col_copies + gather_copies:
         c.wait_send()
-    for c in (cost_out, right_out, left_out, weight_out):
-        c.wait()
 
 
 def on_device(nrow, ncol, left, right, weight, cotangent):
@@ -421,7 +414,7 @@
         jax.ShapeDtypeStruct(right.shape, BF),
     )
     args = (left, right, jnp.swapaxes(weight, 3, 4), jnp.swapaxes(cotangent, 2, 3))
-    scratch = [pltpu.VMEM(a.shape, a.dtype) for a in args + outs] + [
+    scratch = [pltpu.VMEM(a.shape, a.dtype) for a in args] + [
         pltpu.VMEM((rows, 96, channels), BF),
         pltpu.VMEM((rows, 160, channels), F32),
         pltpu.VMEM((rows, 160, channels), F32),
@@ -430,7 +423,7 @@
         pltpu.VMEM((9 * LANES, LANES), BF),
         pltpu.VMEM((9 * LANES, LANES), BF),
         body, body,
-        pltpu.VMEM((WINDOWS, LANES, cells), BF),
+        pltpu.VMEM((LANES, WINDOWS * cells), BF),
         edge, edge, halo, halo,
         pltpu.VMEM((WINDOWS, cells, LANES), BF),
         pltpu.VMEM((2, cells, channels), F32),
@@ -447,22 +440,24 @@
         pltpu.VMEM((2, nrow, slab, 128), BF),
         pltpu.VMEM((2 * halfrows, 128), F32),
         pltpu.VMEM((WINDOWS, cells, LANES), F32),
-        dma((4,)), dma((4,)), dma((4,)), dma((3,)), dma((8,)), dma((8,)), dma((8,)), dma((8,)),
+        dma((4,)), dma((4,)), dma((3,)), dma((8,)), dma((8,)), dma((8,)), dma((8,)),
         dma((2,)), dma((2,)), dma((4,)),
         dma((nrow,)), dma((nrow,)), dma((ncol // 2,)), dma((ncol // 2,)), dma((nrow,)), dma((nrow,)),
     ]
     anywhere = pl.BlockSpec(memory_space=pl.ANY)
-    cost, weight_grad, left_grad, right_grad = pl.pallas_call(
+    vmem = pl.BlockSpec(memory_space=pltpu.VMEM)
+    results = pl.pallas_call(
         functools.partial(kernel, nrow, ncol, scale),
-        out_shape=outs,
+        out_shape=tuple(pltpu.VMEM(a.shape, a.dtype) for a in outs),
         in_specs=[anywhere] * 4,
-        out_specs=(anywhere,) * 4,
+        out_specs=(vmem,) * 4,
         scratch_shapes=scratch,
         compiler_params=pltpu.CompilerParams(
             collective_id=0, has_side_effects=True, vmem_limit_bytes=56 * 1024 * 1024
         ),
         name="cost_volume",
     )(*args)
+    cost, weight_grad, left_grad, right_grad = results
     return jnp.swapaxes(cost, 2, 3), jnp.swapaxes(weight_grad, 3, 4), left_grad, right_grad
 
 

time: 57.2 us -> 48.4 us (0.85)
  Pallas kernels: 51.5 us -> 44.7 us
  local copies, waits for them, and re-layouts: 4.9 us -> 3 us
    pallas_call x1, Pallas kernels: 51.5 us -> 44.7 us  [on_device(): pl.pallas_call(functools.partial(kernel, nrow, ncol, scale), out_shape=tu...]
    unnamed x10 -> x4, local copies, waits for them, and re-layouts: 4.9 us -> 3 us
where the time goes in v4:
time: 48.4 us; the launch traced here: 48.3 us
  Pallas kernels  44.7 us (92%)
  local copies, waits for them, and re-layouts  3 us (6%)
  between operations  0.64 us (1%)
    pallas_call x1, Pallas kernels, on_device(): pl.pallas_call(functools.partial(kernel, nrow, ncol, scale), out_shape=tu...  44.7 us
    unnamed x4, local copies, waits for them, and re-layouts  3 us

profile of v4, /device:TPU:1, one launch (start us, length us, event | category | flops | bytes accessed | tf_op | source)
XLA Modules:
  0.0 48.3 jit_solution(966064158722366784)
XLA Ops:
  0.6 44.7 %cost_volume.1 = (bf16[24,4,32,64]{3,2,1,0:T(8,128)(2,1)S(1)}, f32[3,3,3,32,40]{4,3,2,1,0:T(8,128)S(1)}, bf16[4,64,320]{2,1,0:T(8,128)(2,1)S(1)}, bf16[4,64,320]{2,1,0:T(8,128)(2,1)S(1)}) custom-call(bf16[4,64,320]{2,1,0:T(8,128)(2,1)} %l_any.1, bf16[4,64,320]{2,1,0:T(8,128)(2,1)} %r_any.1, bf16[3,3,3,32,40]{4,3,2,1,0:T(8,128)(2,1)} %bitcast.7, ...), custom_call_target="tpu_custom_call" | custom-call | tf_op jit(solution)/shard_map/cost_volume/pallas_call | solution.py:449
  45.3 0.9 %copy.12 = bf16[24,4,64,32]{2,3,1,0:T(8,128)(2,1)} copy(bf16[24,4,64,32]{2,3,1,0:T(8,128)(2,1)S(1)} %bitcast.4) | data formatting | bytes 786432
  46.2 0.8 %copy.13 = f32[3,3,3,40,32]{3,4,2,1,0:T(8,128)} copy(f32[3,3,3,40,32]{3,4,2,1,0:T(8,128)S(1)} %bitcast.5) | data formatting | bytes 276480
  47.0 0.7 %copy.14 = bf16[4,64,320]{2,1,0:T(8,128)(2,1)} copy(bf16[4,64,320]{2,1,0:T(8,128)(2,1)S(1)} %get-tuple-element.14) | data formatting | bytes 327680
  47.6 0.7 %copy.15 = bf16[4,64,320]{2,1,0:T(8,128)(2,1)} copy(bf16[4,64,320]{2,1,0:T(8,128)(2,1)S(1)} %get-tuple-element.15) | data formatting | bytes 327680

commit v5 on v4

--- a/solution.py
+++ b/solution.py
@@ -33,7 +33,7 @@
     l_any, r_any, w_any, c_any,
     cost_ref, wg_ref, lg_ref, rg_ref,
     l_ref, r_ref, w_ref, c_ref,
-    rband, rf0, rf4, lf, sel, band_n, band_t, cs, vs, vt, edge_c, edge_v, halo_c, halo_v,
+    rband, rf0, rf4, lf, sel, band_n, band_t, cs, vs, vt, edge_c, edge_v, halo_c, halo_v, line_send, line_recv,
     gv, spread, racc0, racc4, back_send, back_recv, dsum, slot_c, half, slots_r, part_m, slots_m,
     gathered, full, obuf,
     sem_in, sem_rs, sem_rr, sem_cs, sem_cr, sem_vs, sem_vr, sem_bs, sem_br, sem_pair,
@@ -53,20 +53,24 @@
     def at(dr, dc):
         return (lax.rem(row + dr + nrow, nrow), lax.rem(col + dc + ncol, ncol))
 
+    def at_mate(step):
+        return (lax.rem(row + step, nrow), mate[1])
+
     def along(step):
         return (row, lax.rem(pair + step, pairs) * 2 + core)
 
     barrier = pltpu.get_barrier_semaphore()
     partners = [at(dr, dc) for dr, dc in NEIGHBOURS if dc != 0]
     partners += [at(step, 0) for step in range(1, nrow)] + [along(step) for step in range(1, pairs)]
-    for partner in partners:
-        pl.semaphore_signal(barrier, inc=1, device_id=partner, device_id_type=MESH)
     loads = [
         pltpu.make_async_copy(src, dst, sem_in.at[n])
         for n, (src, dst) in enumerate(((c_any, c_ref), (w_any, w_ref), (l_any, l_ref), (r_any, r_ref)))
     ]
     for load in loads:
         load.start()
+    partners += [at_mate(step) for step in range(1, nrow)]
+    for partner in partners:
+        pl.semaphore_signal(barrier, inc=1, device_id=partner, device_id_type=MESH)
     pl.semaphore_wait(barrier, len(partners))
 
     def copy(src, dst, send, recv, target):
@@ -87,10 +91,13 @@
     def _():
         beyond.start()
 
-    def halo_copies(body, edge, halo, send, recv):
+    def halo_copies(body, edge, halo, send, recv, lines=None):
         out = []
         for n, (dr, dc) in enumerate(NEIGHBOURS):
-            if dc == 0:
+            if dc == 0 and lines is not None:
+                src = lines[0].at[1 if dr == 1 else 0]
+                dst = lines[1].at[0 if dr == 1 else 1]
+            elif dc == 0:
                 src = body.at[1, :, rows if dr == 1 else 1]
                 dst = body.at[1, :, 0 if dr == 1 else rows + 1]
             else:
@@ -150,9 +157,9 @@
                 parts.append(c_ref[d, h] if 0 <= d < DISP else jnp.zeros((feats, cols), BF))
             cs[1, k, 1 + h] = jnp.concatenate(parts, axis=0).T
     fill_edges(edge_c, cs)
-    cot_copies = halo_copies(cs, edge_c, halo_c, sem_cs, sem_cr)
-    for c in cot_copies:
-        c.start()
+    for side, h in enumerate((0, rows - 1)):
+        line_send[side] = jnp.concatenate([c_ref[d, h] for d in range(DISP)], axis=0).T
+    cot_copies = halo_copies(cs, edge_c, halo_c, sem_cs, sem_cr, (line_send, line_recv))
 
     loads[1].wait()
     loads[2].wait()
@@ -209,6 +216,8 @@
     def _():
         forward_near.start()
 
+    for c in cot_copies:
+        c.start()
     widen(64, col > 0)
     lax.fori_loop(0, 1, volume, 0)
     middle.wait_recv()
@@ -224,6 +233,17 @@
 
     for c in cot_copies:
         c.wait_recv()
+    for side, h in enumerate((0, rows + 1)):
+        line = line_recv[side]
+        blank = jnp.zeros((cols, feats), BF)
+        for k in range(WINDOWS):
+            lo, hi = feats * (OUT_D * k - 1), feats * (OUT_D * k + OUT_D + 1)
+            piece = line[:, max(lo, 0) : min(hi, feats * DISP)]
+            if k == 0:
+                piece = jnp.concatenate([blank, piece], axis=1)
+            if k == WINDOWS - 1:
+                piece = jnp.concatenate([piece, blank], axis=1)
+            cs[1, k, h] = piece
     clear_outside(cs, halo_c)
     write_shifts(cs, halo_c)
 
@@ -340,10 +360,13 @@
         total = total + slots_m[q].astype(F32)
     gathered[core, row] = (total * scale).astype(BF)
     gather_copies = []
-    for step in range(1, nrow):
-        mine = gathered.at[core, row]
-        gather_copies.append(copy(mine, mine, sem3_s.at[step], sem3_r.at[row], at(step, 0)))
-        gather_copies[-1].start()
+    mine = gathered.at[core, row]
+    for step in range(nrow):
+        if step:
+            gather_copies.append(copy(mine, mine, sem3_s.at[0, step], sem3_r.at[core, row], at(step, 0)))
+        gather_copies.append(copy(mine, mine, sem3_s.at[1, step], sem3_r.at[core, row], at_mate(step)))
+    for c in gather_copies:
+        c.start()
 
     lax.fori_loop(2, WINDOWS, forward, 0)
 
@@ -367,13 +390,13 @@
         rg_ref[h, 0:32] = (own[0:32] * inv).astype(BF)
         rg_ref[h, 32:64] = (last * inv).astype(BF)
 
-    for step in range(1, nrow):
-        r = at(step, 0)[0]
-        theirs = gathered.at[core, r]
-        copy(theirs, theirs, sem3_s.at[step], sem3_r.at[r], at(step, 0)).wait_recv()
-    mate_copy = copy(gathered.at[core], gathered.at[core], sem_pair.at[2], sem_pair.at[3], mate)
-    mate_copy.start()
-    mate_copy.wait_recv()
+    for step in range(nrow):
+        r = lax.rem(row + step, nrow)
+        if step:
+            theirs = gathered.at[core, r]
+            copy(theirs, theirs, sem3_s.at[0, step], sem3_r.at[core, r], at(step, 0)).wait_recv()
+        theirs = gathered.at[1 - core, r]
+        copy(theirs, theirs, sem3_s.at[1, step], sem3_r.at[1 - core, r], at_mate(step)).wait_recv()
     for side in range(2):
         for r in range(nrow):
             start = side * halfrows + r * chunk
@@ -390,7 +413,7 @@
         beyond.wait_send()
         forward_near.wait_send()
 
-    sent = [near, middle, pair_copy, mate_copy] + cot_copies + vol_copies + back_copies
+    sent = [near, middle, pair_copy] + cot_copies + vol_copies + back_copies
     for c in sent + row_copies + col_copies + gather_copies:
         c.wait_send()
 
@@ -407,6 +430,7 @@
     body = pltpu.VMEM((3, WINDOWS, rows + 2, cols, LANES), BF)
     edge = pltpu.VMEM((2, 16, LANES), BF)
     halo = pltpu.VMEM((2, 3, 16, LANES), BF)
+    line = pltpu.VMEM((2, cols, DISP * feats), BF)
     outs = (
         jax.ShapeDtypeStruct((DISP, rows, feats, cols), BF),
         jax.ShapeDtypeStruct((3, 3, 3, feats, groups), F32),
@@ -424,7 +448,7 @@
         pltpu.VMEM((9 * LANES, LANES), BF),
         body, body,
         pltpu.VMEM((LANES, WINDOWS * cells), BF),
-        edge, edge, halo, halo,
+        edge, edge, halo, halo, line, line,
         pltpu.VMEM((WINDOWS, cells, LANES), BF),
         pltpu.VMEM((2, cells, channels), F32),
         pltpu.VMEM((rows, 160, channels), F32),
@@ -441,8 +465,8 @@
         pltpu.VMEM((2 * halfrows, 128), F32),
         pltpu.VMEM((WINDOWS, cells, LANES), F32),
         dma((4,)), dma((4,)), dma((3,)), dma((8,)), dma((8,)), dma((8,)), dma((8,)),
-        dma((2,)), dma((2,)), dma((4,)),
-        dma((nrow,)), dma((nrow,)), dma((ncol // 2,)), dma((ncol // 2,)), dma((nrow,)), dma((nrow,)),
+        dma((2,)), dma((2,)), dma((2,)),
+        dma((nrow,)), dma((nrow,)), dma((ncol // 2,)), dma((ncol // 2,)), dma((2, nrow)), dma((2, nrow)),
     ]
     anywhere = pl.BlockSpec(memory_space=pl.ANY)
     vmem = pl.BlockSpec(memory_space=pltpu.VMEM)

time: 48.4 us -> 45.7 us (0.944)
  Pallas kernels: 44.7 us -> 42 us
    pallas_call x1, Pallas kernels: 44.7 us -> 42 us  [on_device(): pl.pallas_call(functools.partial(kernel, nrow, ncol, scale), out_shape=tu...]
where the time goes in v5:
time: 45.7 us
  Pallas kernels  42 us (92%)
  local copies, waits for them, and re-layouts  3 us (7%)
  between operations  0.64 us (1%)
    pallas_call x1, Pallas kernels, on_device(): pl.pallas_call(functools.partial(kernel, nrow, ncol, scale), out_shape=tu...  42 us
    unnamed x4, local copies, waits for them, and re-layouts  3 us

profile of v5, /device:TPU:1, one launch (start us, length us, event | category | flops | bytes accessed | tf_op | source)
XLA Modules:
  0.0 45.7 jit_solution(13471070542352634386)
XLA Ops:
  0.6 42.0 %cost_volume.1 = (bf16[24,4,32,64]{3,2,1,0:T(8,128)(2,1)S(1)}, f32[3,3,3,32,40]{4,3,2,1,0:T(8,128)S(1)}, bf16[4,64,320]{2,1,0:T(8,128)(2,1)S(1)}, bf16[4,64,320]{2,1,0:T(8,128)(2,1)S(1)}) custom-call(bf16[4,64,320]{2,1,0:T(8,128)(2,1)} %l_any.1, bf16[4,64,320]{2,1,0:T(8,128)(2,1)} %r_any.1, bf16[3,3,3,32,40]{4,3,2,1,0:T(8,128)(2,1)} %bitcast.7, ...), custom_call_target="tpu_custom_call" | custom-call | tf_op jit(solution)/shard_map/cost_volume/pallas_call | solution.py:473
  42.7 0.9 %copy.12 = bf16[24,4,64,32]{2,3,1,0:T(8,128)(2,1)} copy(bf16[24,4,64,32]{2,3,1,0:T(8,128)(2,1)S(1)} %bitcast.4) | data formatting | bytes 786432
  43.6 0.8 %copy.13 = f32[3,3,3,40,32]{3,4,2,1,0:T(8,128)} copy(f32[3,3,3,40,32]{3,4,2,1,0:T(8,128)S(1)} %bitcast.5) | data formatting | bytes 276480
  44.3 0.7 %copy.14 = bf16[4,64,320]{2,1,0:T(8,128)(2,1)} copy(bf16[4,64,320]{2,1,0:T(8,128)(2,1)S(1)} %get-tuple-element.14) | data formatting | bytes 327680
  45.0 0.7 %copy.15 = bf16[4,64,320]{2,1,0:T(8,128)(2,1)} copy(bf16[4,64,320]{2,1,0:T(8,128)(2,1)S(1)} %get-tuple-element.15) | data formatting | bytes 327680

commit v6 on v5

--- a/solution.py
+++ b/solution.py
@@ -84,12 +84,12 @@
     middle = copy(r_any.at[:, 0:32], rband.at[:, 32:64], sem_rs.at[1], sem_rr.at[1], at(0, 1))
     beyond = copy(tail, rband.at[:, 0:32], sem_rs.at[2], sem_rr.at[2], at(0, 2))
     forward_near = copy(rband.at[:, 64:96], rband.at[:, 0:32], sem_rs.at[3], sem_rr.at[2], mate)
-    near.start()
-    middle.start()
-
     @pl.when(core == 0)
     def _():
         beyond.start()
+
+    near.start()
+    middle.start()
 
     def halo_copies(body, edge, halo, send, recv, lines=None):
         out = []

time: 45.7 us -> 45.8 us (level)
  no operation moved by 1% of the time
where the time goes in v6:
time: 45.8 us; the launch traced here: 45.7 us
  Pallas kernels  42 us (92%)
  local copies, waits for them, and re-layouts  3 us (7%)
  between operations  0.64 us (1%)
    pallas_call x1, Pallas kernels, on_device(): pl.pallas_call(functools.partial(kernel, nrow, ncol, scale), out_shape=tu...  42 us
    unnamed x4, local copies, waits for them, and re-layouts  3 us

profile of v6, /device:TPU:1, one launch (start us, length us, event | category | flops | bytes accessed | tf_op | source)
XLA Modules:
  0.0 45.7 jit_solution(4067374529966931436)
XLA Ops:
  0.6 42.0 %cost_volume.1 = (bf16[24,4,32,64]{3,2,1,0:T(8,128)(2,1)S(1)}, f32[3,3,3,32,40]{4,3,2,1,0:T(8,128)S(1)}, bf16[4,64,320]{2,1,0:T(8,128)(2,1)S(1)}, bf16[4,64,320]{2,1,0:T(8,128)(2,1)S(1)}) custom-call(bf16[4,64,320]{2,1,0:T(8,128)(2,1)} %l_any.1, bf16[4,64,320]{2,1,0:T(8,128)(2,1)} %r_any.1, bf16[3,3,3,32,40]{4,3,2,1,0:T(8,128)(2,1)} %bitcast.7, ...), custom_call_target="tpu_custom_call" | custom-call | tf_op jit(solution)/shard_map/cost_volume/pallas_call | solution.py:473
  42.7 0.9 %copy.12 = bf16[24,4,64,32]{2,3,1,0:T(8,128)(2,1)} copy(bf16[24,4,64,32]{2,3,1,0:T(8,128)(2,1)S(1)} %bitcast.4) | data formatting | bytes 786432
  43.6 0.8 %copy.13 = f32[3,3,3,40,32]{3,4,2,1,0:T(8,128)} copy(f32[3,3,3,40,32]{3,4,2,1,0:T(8,128)S(1)} %bitcast.5) | data formatting | bytes 276480
  44.3 0.7 %copy.14 = bf16[4,64,320]{2,1,0:T(8,128)(2,1)} copy(bf16[4,64,320]{2,1,0:T(8,128)(2,1)S(1)} %get-tuple-element.14) | data formatting | bytes 327680
  45.0 0.7 %copy.15 = bf16[4,64,320]{2,1,0:T(8,128)(2,1)} copy(bf16[4,64,320]{2,1,0:T(8,128)(2,1)S(1)} %get-tuple-element.15) | data formatting | bytes 327680

commit v7 on v6

--- a/solution.py
+++ b/solution.py
@@ -350,7 +350,7 @@
         obuf[k] = dot(jnp.concatenate(taps, axis=1), band_n[...])
         return carry
 
-    lax.fori_loop(0, 2, forward, 0)
+    lax.fori_loop(0, 1, forward, 0)
 
     for step in range(1, pairs):
         p = lax.rem(pair + step, pairs)
@@ -368,7 +368,7 @@
     for c in gather_copies:
         c.start()
 
-    lax.fori_loop(2, WINDOWS, forward, 0)
+    lax.fori_loop(1, WINDOWS, forward, 0)
 
     for h in range(rows):
         part = [obuf[k, cols * h : cols * (h + 1)].T for k in range(WINDOWS)]

time: 45.8 us -> 45.8 us (level)
  no operation moved by 1% of the time
where the time goes in v7:
time: 45.8 us; the launch traced here: 45.7 us
  Pallas kernels  42 us (92%)
  local copies, waits for them, and re-layouts  3 us (7%)
  between operations  0.64 us (1%)
    pallas_call x1, Pallas kernels, on_device(): pl.pallas_call(functools.partial(kernel, nrow, ncol, scale), out_shape=tu...  42 us
    unnamed x4, local copies, waits for them, and re-layouts  3 us

profile of v7, /device:TPU:1, one launch (start us, length us, event | category | flops | bytes accessed | tf_op | source)
XLA Modules:
  0.0 45.7 jit_solution(8590048457659747274)
XLA Ops:
  0.6 42.0 %cost_volume.1 = (bf16[24,4,32,64]{3,2,1,0:T(8,128)(2,1)S(1)}, f32[3,3,3,32,40]{4,3,2,1,0:T(8,128)S(1)}, bf16[4,64,320]{2,1,0:T(8,128)(2,1)S(1)}, bf16[4,64,320]{2,1,0:T(8,128)(2,1)S(1)}) custom-call(bf16[4,64,320]{2,1,0:T(8,128)(2,1)} %l_any.1, bf16[4,64,320]{2,1,0:T(8,128)(2,1)} %r_any.1, bf16[3,3,3,32,40]{4,3,2,1,0:T(8,128)(2,1)} %bitcast.7, ...), custom_call_target="tpu_custom_call" | custom-call | tf_op jit(solution)/shard_map/cost_volume/pallas_call | solution.py:473
  42.7 0.9 %copy.12 = bf16[24,4,64,32]{2,3,1,0:T(8,128)(2,1)} copy(bf16[24,4,64,32]{2,3,1,0:T(8,128)(2,1)S(1)} %bitcast.4) | data formatting | bytes 786432
  43.6 0.8 %copy.13 = f32[3,3,3,40,32]{3,4,2,1,0:T(8,128)} copy(f32[3,3,3,40,32]{3,4,2,1,0:T(8,128)S(1)} %bitcast.5) | data formatting | bytes 276480
  44.3 0.7 %copy.14 = bf16[4,64,320]{2,1,0:T(8,128)(2,1)} copy(bf16[4,64,320]{2,1,0:T(8,128)(2,1)S(1)} %get-tuple-element.14) | data formatting | bytes 327680
  45.0 0.7 %copy.15 = bf16[4,64,320]{2,1,0:T(8,128)(2,1)} copy(bf16[4,64,320]{2,1,0:T(8,128)(2,1)S(1)} %get-tuple-element.15) | data formatting | bytes 327680
